TPU v7x, 128 devices: a whole 4x4x4 slice. The times are simulated.
128 devices in a mesh: seq: 8 (over x_lo, z), chan: 16 (over x_hi, y, core).
Axes of the slice: x: 4 (x_hi: 2, x_lo: 2; x = x_hi * 2 + x_lo), y: 4, z: 4, core: 2. Of those that a mesh axis runs over, the one named last changes fastest.
Arguments:
- projections: bfloat16 [3, 256, 32768], P(None, None, ('seq', 'chan')), may hold values from -6 to 6
- taps: float32 [3, 256, 3], replicated, may hold values from -2.4 to 2.4
- filter_spectra: float32 [256, 64, 2, 1024], P('chan'), may hold values from -1.2 to 1.2
- skip_gain: float32 [256], replicated, may hold values from -3 to 3
Outputs:
- gated: bfloat16 [256, 32768], P('chan', 'seq')
All inputs are finite; a program needn't handle non-finite values.
Results may differ from a plain program's by a relative error of at most 0.001.
Values may be sent and summed in bfloat16 or wider, within the bound.
No kernel may reach another device: no remote copies, remote signals or barrier semaphores. Data moves between devices by JAX's collectives and lax.ppermute only.
A program may use at most 64 MiB of HBM per device.

v0:
```python
import math

import jax
import jax.numpy as jnp
from jax import lax
from jax.sharding import PartitionSpec as P


def from_behind(value, axis, steps):
    count = lax.axis_size(axis)
    first, last = (max(0, -steps), min(count, count - steps))
    return lax.ppermute(value, axis, [(source, source + steps) for source in range(first, last)])


def convolve(rows, before_rows, weights):
    joined = jnp.concatenate([before_rows, rows], axis=2).astype(jnp.float32)
    count = rows.shape[2]
    width = weights.shape[2]
    total = jnp.zeros(rows.shape, jnp.float32)
    for shift_at in range(width):
        start = width - 1 - shift_at
        total = total + weights[:, :, shift_at : shift_at + 1] * joined[:, :, start : start + count]
    return total


def body(projections, taps, filter_spectra, skip_gain):
    chan_count = lax.axis_size("chan")
    local_chan = projections.shape[1] // chan_count
    offset = lax.axis_index("chan") * local_chan
    my_gain = lax.dynamic_slice_in_dim(skip_gain, offset, local_chan, 0)
    edge = taps.shape[2] - 1
    before_rows = from_behind(projections[:, :, projections.shape[2] - edge :], ("seq", "chan"), 1)
    featured = convolve(projections, before_rows, taps)
    local = lax.all_to_all(featured, "chan", split_axis=1, concat_axis=2, tiled=True)
    query, key, value = (local[0], local[1], local[2])
    product = key * value
    block_len = product.shape[1]
    sub = filter_spectra.shape[3] // 2
    freq = 2 * sub
    blocks = block_len // sub
    highest = lax.Precision.HIGHEST
    tau = lax.broadcasted_iota(jnp.int32, (sub, freq), 0)
    fre = lax.broadcasted_iota(jnp.int32, (sub, freq), 1)
    phase = (tau * fre % freq).astype(jnp.float32) * (2.0 * math.pi / freq)
    cosine = jnp.cos(phase)
    sine = jnp.sin(phase)
    lead_zeros = jnp.zeros((local_chan, blocks - 1, freq), jnp.float32)
    filter_real = jnp.concatenate([lead_zeros, filter_spectra[:, :, 0, :]], axis=1)
    filter_imag = jnp.concatenate([lead_zeros, filter_spectra[:, :, 1, :]], axis=1)

    def spectrum(block):
        rows = block.reshape(local_chan, blocks, sub)
        real_part = jnp.einsum("cnt,tf->cnf", rows, cosine, precision=highest)
        imag_part = -jnp.einsum("cnt,tf->cnf", rows, sine, precision=highest)
        return (real_part, imag_part)

    def accumulate(step, real_part, imag_part, acc_real, acc_imag):

        def add_source(source, totals):
            sum_real, sum_imag = totals
            start = step * blocks + blocks - 1 - source
            lag_real = lax.dynamic_slice_in_dim(filter_real, start, blocks, 1)
            lag_imag = lax.dynamic_slice_in_dim(filter_imag, start, blocks, 1)
            src_real = lax.dynamic_slice_in_dim(real_part, source, 1, 1)
            src_imag = lax.dynamic_slice_in_dim(imag_part, source, 1, 1)
            sum_real = sum_real + (lag_real * src_real - lag_imag * src_imag)
            sum_imag = sum_imag + (lag_real * src_imag + lag_imag * src_real)
            return (sum_real, sum_imag)

        return lax.fori_loop(0, blocks, add_source, (acc_real, acc_imag))

    seq_count = lax.axis_size("seq")
    zeros = jnp.zeros((local_chan, blocks, freq), jnp.float32)

    def turn_blocks(step, carry):
        block, acc_real, acc_imag = carry
        real_part, imag_part = spectrum(block)
        acc_real, acc_imag = accumulate(step, real_part, imag_part, acc_real, acc_imag)
        block = from_behind(block, "seq", 1)
        return (block, acc_real, acc_imag)

    block, acc_real, acc_imag = lax.fori_loop(
        0, seq_count - 1, turn_blocks, (product, zeros, zeros)
    )
    real_part, imag_part = spectrum(block)
    acc_real, acc_imag = accumulate(seq_count - 1, real_part, imag_part, acc_real, acc_imag)
    long_part = (
        jnp.einsum("cnf,tf->cnt", acc_real, cosine, precision=highest)
        - jnp.einsum("cnf,tf->cnt", acc_imag, sine, precision=highest)
    ) / freq
    long_part = long_part.reshape(local_chan, block_len)
    return (query * (long_part + my_gain[:, None] * product)).astype(jnp.bfloat16)


def solution(mesh):
    placed = (P(None, None, ("seq", "chan")), P(), P("chan", None, None, None), P())
    return jax.shard_map(
        body, mesh=mesh, in_specs=placed, out_specs=P("chan", "seq"), check_vma=False
    )
```

profile of v0, /device:TPU:0, one launch (start us, length us, event | category | flops | bytes accessed | tf_op | source)
XLA Modules:
  0.0 387.4 jit_solution(3369311302626362238)
XLA Ops:
  4.8 2.9 fusion.54
  7.7 13.2 %all-to-all-start = ((f32[3,256,256]{2,0,1:T(4,128)}), f32[3,256,256]{2,0,1:T(4,128)S(1)}, u32[]{:S(2)}, u32[]{:S(2)}) async-start(f32[3,256,256]{2,0,1:T(4,128)} %fusion.54), calls=%async_computation | async-start | bytes 2097152 | tf_op jit(solution)/shard_map/all_to_all | solution.py:34
  20.9 11.4 %fusion.80 = (f32[16,64,1,1024]{3,2,1,0:T(1,128)}, f32[16,64,1,1024]{3,2,1,0:T(1,128)}) fusion(f32[16,64,2,1024]{3,2,1,0:T(2,128)} %param.12), kind=kLoop, calls=%fused_computation.88 | loop fusion | bytes 16777216 | tf_op jit(solution)/shard_map/slice | solution.py:49
  32.3 5.5 %copy_bitcast_fusion.2 = (f32[16,64,1024]{2,1,0:T(8,128)S(1)}, f32[16,64,1024]{2,1,0:T(8,128)S(1)}) fusion(f32[16,64,1,1024]{3,2,1,0:T(1,128)} %get-tuple-element.838, f32[16,64,1,1024]{3,2,1,0:T(1,128)} %get-tuple-element.839), kind=kLoop, calls=%fused_computation.38 | loop fusion | bytes 16777216 | tf_op jit(solution)/shard_map/squeeze | solution.py:49
  37.8 2.7 concatenate.10
  40.6 2.8 concatenate.11
  44.4 284.3 %while.77 = (s32[]{:T(128)}, f32[16,4096]{1,0:T(8,128)S(1)}, f32[16,8,1024]{2,1,0:T(8,128)S(1)}, f32[16,8,1024]{2,1,0:T(8,128)S(1)}, f32[16,71,1024]{2,1,0:T(8,1...) while((s32[]{:T(128)}, f32[16,4096]{1,0:T(8,128)S(1)}, ...), condition=%wide.region_3.4_spmd.clone, body=%wide.region_0.3_spmd.clone.sunk | while | flops 1626472448 | bytes 7340484 | solution.py:82
  44.4 4.2 %collective-permute-start = (f32[16,4096]{1,0:T(8,128)S(1)}, f32[16,4096]{1,0:T(8,128)S(1)}, u32[]{:S(2)}, u32[]{:S(2)}) collective-permute-start(f32[16,4096]{1,0:T(8,128)S(1)} %copy.111), channel_id=1, source_target_pairs={{0,16},{16,32},{32,48},{48,64},{64,80},{80,96},{96,112},{1,17},{17... | collective-permute-start | bytes 786440 | tf_op jit(solution)/shard_map/while/body/eval_jaxpr/ppermute | solution.py:12
  48.8 9.7 %fusion.97 = f32[16,8,1024]{2,1,0:T(8,128)S(1)} fusion(f32[16,8,512]{2,1,0:T(8,128)S(1)} %bitcast.88), kind=kOutput, calls=%fused_computation.27.clone.1 | convolution fusion | flops 812777472 | bytes 786432 | tf_op jit(solution)/shard_map/while/body/eval_jaxpr/cnt,tf->cnf/dot_general | solution.py:54
  58.5 9.7 %fusion.96 = f32[16,8,1024]{2,0,1:T(8,128)S(1)} fusion(f32[2,8,8,512]{3,2,1,0:T(8,128)S(1)} %bitcast.85), kind=kOutput, calls=%fused_computation.20.clone.1 | convolution fusion | flops 812646400 | bytes 786432 | tf_op jit(solution)/shard_map/while/body/eval_jaxpr/cnt,tf->cnf/dot_general | solution.py:53
  68.2 17.4 %while.78 = (s32[]{:T(128)}, f32[16,8,1024]{2,1,0:T(8,128)S(1)}, f32[16,8,1024]{2,1,0:T(8,128)S(1)}, s32[]{:T(128)}, f32[16,71,1024]{2,1,0:T(8,128)}, /*index=5*...) while((s32[]{:T(128)}, f32[16,8,1024]{2,1,0:T(8,128)S(1)}, ...), condition=%wide.region_2.2_spmd, body=%wide.region_1.1_spmd.sunk | while | flops 1048582 | bytes 3670183 | solution.py:70
  85.7 3.8 collective-permute-start
  89.7 9.7 %fusion.97 = f32[16,8,1024]{2,1,0:T(8,128)S(1)} fusion(f32[16,8,512]{2,1,0:T(8,128)S(1)} %bitcast.88), kind=kOutput, calls=%fused_computation.27.clone.1 | convolution fusion | flops 812777472 | bytes 786432 | tf_op jit(solution)/shard_map/while/body/eval_jaxpr/cnt,tf->cnf/dot_general | solution.py:54
  99.4 9.7 %fusion.96 = f32[16,8,1024]{2,0,1:T(8,128)S(1)} fusion(f32[2,8,8,512]{3,2,1,0:T(8,128)S(1)} %bitcast.85), kind=kOutput, calls=%fused_computation.20.clone.1 | convolution fusion | flops 812646400 | bytes 786432 | tf_op jit(solution)/shard_map/while/body/eval_jaxpr/cnt,tf->cnf/dot_general | solution.py:53
  109.1 17.4 %while.78 = (s32[]{:T(128)}, f32[16,8,1024]{2,1,0:T(8,128)S(1)}, f32[16,8,1024]{2,1,0:T(8,128)S(1)}, s32[]{:T(128)}, f32[16,71,1024]{2,1,0:T(8,128)}, /*index=5*...) while((s32[]{:T(128)}, f32[16,8,1024]{2,1,0:T(8,128)S(1)}, ...), condition=%wide.region_2.2_spmd, body=%wide.region_1.1_spmd.sunk | while | flops 1048582 | bytes 3670183 | solution.py:70
  126.6 3.5 collective-permute-start
  130.3 9.7 %fusion.97 = f32[16,8,1024]{2,1,0:T(8,128)S(1)} fusion(f32[16,8,512]{2,1,0:T(8,128)S(1)} %bitcast.88), kind=kOutput, calls=%fused_computation.27.clone.1 | convolution fusion | flops 812777472 | bytes 786432 | tf_op jit(solution)/shard_map/while/body/eval_jaxpr/cnt,tf->cnf/dot_general | solution.py:54
  140.0 9.7 %fusion.96 = f32[16,8,1024]{2,0,1:T(8,128)S(1)} fusion(f32[2,8,8,512]{3,2,1,0:T(8,128)S(1)} %bitcast.85), kind=kOutput, calls=%fused_computation.20.clone.1 | convolution fusion | flops 812646400 | bytes 786432 | tf_op jit(solution)/shard_map/while/body/eval_jaxpr/cnt,tf->cnf/dot_general | solution.py:53
  149.7 17.4 %while.78 = (s32[]{:T(128)}, f32[16,8,1024]{2,1,0:T(8,128)S(1)}, f32[16,8,1024]{2,1,0:T(8,128)S(1)}, s32[]{:T(128)}, f32[16,71,1024]{2,1,0:T(8,128)}, /*index=5*...) while((s32[]{:T(128)}, f32[16,8,1024]{2,1,0:T(8,128)S(1)}, ...), condition=%wide.region_2.2_spmd, body=%wide.region_1.1_spmd.sunk | while | flops 1048582 | bytes 3670183 | solution.py:70
  167.2 2.6 collective-permute-start
  170.0 9.7 %fusion.97 = f32[16,8,1024]{2,1,0:T(8,128)S(1)} fusion(f32[16,8,512]{2,1,0:T(8,128)S(1)} %bitcast.88), kind=kOutput, calls=%fused_computation.27.clone.1 | convolution fusion | flops 812777472 | bytes 786432 | tf_op jit(solution)/shard_map/while/body/eval_jaxpr/cnt,tf->cnf/dot_general | solution.py:54
  179.7 9.7 %fusion.96 = f32[16,8,1024]{2,0,1:T(8,128)S(1)} fusion(f32[2,8,8,512]{3,2,1,0:T(8,128)S(1)} %bitcast.85), kind=kOutput, calls=%fused_computation.20.clone.1 | convolution fusion | flops 812646400 | bytes 786432 | tf_op jit(solution)/shard_map/while/body/eval_jaxpr/cnt,tf->cnf/dot_general | solution.py:53
  189.4 17.4 %while.78 = (s32[]{:T(128)}, f32[16,8,1024]{2,1,0:T(8,128)S(1)}, f32[16,8,1024]{2,1,0:T(8,128)S(1)}, s32[]{:T(128)}, f32[16,71,1024]{2,1,0:T(8,128)}, /*index=5*...) while((s32[]{:T(128)}, f32[16,8,1024]{2,1,0:T(8,128)S(1)}, ...), condition=%wide.region_2.2_spmd, body=%wide.region_1.1_spmd.sunk | while | flops 1048582 | bytes 3670183 | solution.py:70
  189.5 2.1 add_add_fusion.5
  191.7 2.1 add_add_fusion.5
  193.9 2.1 add_add_fusion.5
  196.1 2.1 add_add_fusion.5
  198.3 2.1 add_add_fusion.5
  200.4 2.1 add_add_fusion.5
  202.6 2.1 add_add_fusion.5
  204.8 2.1 add_add_fusion.5
  206.9 3.2 collective-permute-start
  210.3 9.7 %fusion.97 = f32[16,8,1024]{2,1,0:T(8,128)S(1)} fusion(f32[16,8,512]{2,1,0:T(8,128)S(1)} %bitcast.88), kind=kOutput, calls=%fused_computation.27.clone.1 | convolution fusion | flops 812777472 | bytes 786432 | tf_op jit(solution)/shard_map/while/body/eval_jaxpr/cnt,tf->cnf/dot_general | solution.py:54
  220.0 9.7 %fusion.96 = f32[16,8,1024]{2,0,1:T(8,128)S(1)} fusion(f32[2,8,8,512]{3,2,1,0:T(8,128)S(1)} %bitcast.85), kind=kOutput, calls=%fused_computation.20.clone.1 | convolution fusion | flops 812646400 | bytes 786432 | tf_op jit(solution)/shard_map/while/body/eval_jaxpr/cnt,tf->cnf/dot_general | solution.py:53
  229.7 17.4 %while.78 = (s32[]{:T(128)}, f32[16,8,1024]{2,1,0:T(8,128)S(1)}, f32[16,8,1024]{2,1,0:T(8,128)S(1)}, s32[]{:T(128)}, f32[16,71,1024]{2,1,0:T(8,128)}, /*index=5*...) while((s32[]{:T(128)}, f32[16,8,1024]{2,1,0:T(8,128)S(1)}, ...), condition=%wide.region_2.2_spmd, body=%wide.region_1.1_spmd.sunk | while | flops 1048582 | bytes 3670183 | solution.py:70
  247.2 3.8 collective-permute-start
  251.2 9.7 %fusion.97 = f32[16,8,1024]{2,1,0:T(8,128)S(1)} fusion(f32[16,8,512]{2,1,0:T(8,128)S(1)} %bitcast.88), kind=kOutput, calls=%fused_computation.27.clone.1 | convolution fusion | flops 812777472 | bytes 786432 | tf_op jit(solution)/shard_map/while/body/eval_jaxpr/cnt,tf->cnf/dot_general | solution.py:54
  260.9 9.7 %fusion.96 = f32[16,8,1024]{2,0,1:T(8,128)S(1)} fusion(f32[2,8,8,512]{3,2,1,0:T(8,128)S(1)} %bitcast.85), kind=kOutput, calls=%fused_computation.20.clone.1 | convolution fusion | flops 812646400 | bytes 786432 | tf_op jit(solution)/shard_map/while/body/eval_jaxpr/cnt,tf->cnf/dot_general | solution.py:53
  270.6 17.4 %while.78 = (s32[]{:T(128)}, f32[16,8,1024]{2,1,0:T(8,128)S(1)}, f32[16,8,1024]{2,1,0:T(8,128)S(1)}, s32[]{:T(128)}, f32[16,71,1024]{2,1,0:T(8,128)}, /*index=5*...) while((s32[]{:T(128)}, f32[16,8,1024]{2,1,0:T(8,128)S(1)}, ...), condition=%wide.region_2.2_spmd, body=%wide.region_1.1_spmd.sunk | while | flops 1048582 | bytes 3670183 | solution.py:70
  288.1 3.5 collective-permute-start
  291.8 9.7 %fusion.97 = f32[16,8,1024]{2,1,0:T(8,128)S(1)} fusion(f32[16,8,512]{2,1,0:T(8,128)S(1)} %bitcast.88), kind=kOutput, calls=%fused_computation.27.clone.1 | convolution fusion | flops 812777472 | bytes 786432 | tf_op jit(solution)/shard_map/while/body/eval_jaxpr/cnt,tf->cnf/dot_general | solution.py:54
  301.5 9.7 %fusion.96 = f32[16,8,1024]{2,0,1:T(8,128)S(1)} fusion(f32[2,8,8,512]{3,2,1,0:T(8,128)S(1)} %bitcast.85), kind=kOutput, calls=%fused_computation.20.clone.1 | convolution fusion | flops 812646400 | bytes 786432 | tf_op jit(solution)/shard_map/while/body/eval_jaxpr/cnt,tf->cnf/dot_general | solution.py:53
  311.3 17.4 %while.78 = (s32[]{:T(128)}, f32[16,8,1024]{2,1,0:T(8,128)S(1)}, f32[16,8,1024]{2,1,0:T(8,128)S(1)}, s32[]{:T(128)}, f32[16,71,1024]{2,1,0:T(8,128)}, /*index=5*...) while((s32[]{:T(128)}, f32[16,8,1024]{2,1,0:T(8,128)S(1)}, ...), condition=%wide.region_2.2_spmd, body=%wide.region_1.1_spmd.sunk | while | flops 1048582 | bytes 3670183 | solution.py:70
  328.9 9.9 %fusion.45 = f32[16,8,1024]{2,1,0:T(8,128)S(1)} fusion(f32[16,8,512]{2,1,0:T(8,128)S(1)} %bitcast.100), kind=kOutput, calls=%fused_computation.57 | convolution fusion | flops 812777472 | bytes 786432 | tf_op jit(solution)/shard_map/cnt,tf->cnf/dot_general | solution.py:54
  338.8 9.7 %fusion.40 = f32[16,8,1024]{2,0,1:T(8,128)S(1)} fusion(f32[2,8,8,512]{3,2,1,0:T(8,128)S(1)} %bitcast.87), kind=kOutput, calls=%fused_computation.52 | convolution fusion | flops 812646400 | bytes 786432 | tf_op jit(solution)/shard_map/cnt,tf->cnf/dot_general | solution.py:53
  348.5 17.4 %while.75 = (s32[]{:T(128)}, f32[16,8,1024]{2,1,0:T(8,128)S(1)}, f32[16,8,1024]{2,1,0:T(8,128)S(1)}, f32[16,71,1024]{2,1,0:T(8,128)}, f32[16,8,1024]{2,0,1:T(8,1...) while((s32[]{:T(128)}, f32[16,8,1024]{2,1,0:T(8,128)S(1)}, ...), condition=%wide.region_5.6_spmd, body=%wide.region_4.5_spmd.sunk | while | flops 1048582 | bytes 3670183 | solution.py:70
  365.9 10.0 %fusion.34 = f32[16,8,512]{2,1,0:T(8,128)S(1)} fusion(f32[16,8,1024]{2,1,0:T(8,128)S(1)} %get-tuple-element.695), kind=kOutput, calls=%fused_computation.46 | convolution fusion | flops 812646400 | bytes 786432 | tf_op jit(solution)/shard_map/cnf,tf->cnt/dot_general | solution.py:89
  375.9 10.2 %fusion.51 = f32[16,8,512]{2,1,0:T(8,128)S(1)} fusion(f32[16,8,512]{2,1,0:T(8,128)S(1)} %fusion.34, f32[16,8,1024]{2,1,0:T(8,128)S(1)} %get-tuple-element.694), kind=kOutput, calls=%fused_computation.59 | convolution fusion | flops 812777472 | bytes 1048576 | tf_op jit(solution)/shard_map/cnf,tf->cnt/dot_general | solution.py:88
  (229 shorter events, 128.8 us)
Async XLA Ops:
  1.5 2.6 collective-permute-start.1
  7.7 35.7 %all-to-all-start = ((f32[3,256,256]{2,0,1:T(4,128)}), f32[3,256,256]{2,0,1:T(4,128)S(1)}, u32[]{:S(2)}, u32[]{:S(2)}) async-start(f32[3,256,256]{2,0,1:T(4,128)} %fusion.54), calls=%async_computation | async-start | bytes 2097152 | tf_op jit(solution)/shard_map/all_to_all | solution.py:34
  40.6 2.8 copy-start
  44.4 41.2 %collective-permute-start = (f32[16,4096]{1,0:T(8,128)S(1)}, f32[16,4096]{1,0:T(8,128)S(1)}, u32[]{:S(2)}, u32[]{:S(2)}) collective-permute-start(f32[16,4096]{1,0:T(8,128)S(1)} %copy.111), channel_id=1, source_target_pairs={{0,16},{16,32},{32,48},{48,64},{64,80},{80,96},{96,112},{1,17},{17... | collective-permute-start | bytes 786440 | tf_op jit(solution)/shard_map/while/body/eval_jaxpr/ppermute | solution.py:12
  85.7 40.9 %collective-permute-start = (f32[16,4096]{1,0:T(8,128)S(1)}, f32[16,4096]{1,0:T(8,128)S(1)}, u32[]{:S(2)}, u32[]{:S(2)}) collective-permute-start(f32[16,4096]{1,0:T(8,128)S(1)} %copy.111), channel_id=1, source_target_pairs={{0,16},{16,32},{32,48},{48,64},{64,80},{80,96},{96,112},{1,17},{17... | collective-permute-start | bytes 786440 | tf_op jit(solution)/shard_map/while/body/eval_jaxpr/ppermute | solution.py:12
  126.6 40.6 %collective-permute-start = (f32[16,4096]{1,0:T(8,128)S(1)}, f32[16,4096]{1,0:T(8,128)S(1)}, u32[]{:S(2)}, u32[]{:S(2)}) collective-permute-start(f32[16,4096]{1,0:T(8,128)S(1)} %copy.111), channel_id=1, source_target_pairs={{0,16},{16,32},{32,48},{48,64},{64,80},{80,96},{96,112},{1,17},{17... | collective-permute-start | bytes 786440 | tf_op jit(solution)/shard_map/while/body/eval_jaxpr/ppermute | solution.py:12
  167.2 39.7 %collective-permute-start = (f32[16,4096]{1,0:T(8,128)S(1)}, f32[16,4096]{1,0:T(8,128)S(1)}, u32[]{:S(2)}, u32[]{:S(2)}) collective-permute-start(f32[16,4096]{1,0:T(8,128)S(1)} %copy.111), channel_id=1, source_target_pairs={{0,16},{16,32},{32,48},{48,64},{64,80},{80,96},{96,112},{1,17},{17... | collective-permute-start | bytes 786440 | tf_op jit(solution)/shard_map/while/body/eval_jaxpr/ppermute | solution.py:12
  206.9 40.3 %collective-permute-start = (f32[16,4096]{1,0:T(8,128)S(1)}, f32[16,4096]{1,0:T(8,128)S(1)}, u32[]{:S(2)}, u32[]{:S(2)}) collective-permute-start(f32[16,4096]{1,0:T(8,128)S(1)} %copy.111), channel_id=1, source_target_pairs={{0,16},{16,32},{32,48},{48,64},{64,80},{80,96},{96,112},{1,17},{17... | collective-permute-start | bytes 786440 | tf_op jit(solution)/shard_map/while/body/eval_jaxpr/ppermute | solution.py:12
  247.2 40.9 %collective-permute-start = (f32[16,4096]{1,0:T(8,128)S(1)}, f32[16,4096]{1,0:T(8,128)S(1)}, u32[]{:S(2)}, u32[]{:S(2)}) collective-permute-start(f32[16,4096]{1,0:T(8,128)S(1)} %copy.111), channel_id=1, source_target_pairs={{0,16},{16,32},{32,48},{48,64},{64,80},{80,96},{96,112},{1,17},{17... | collective-permute-start | bytes 786440 | tf_op jit(solution)/shard_map/while/body/eval_jaxpr/ppermute | solution.py:12
  288.1 40.6 %collective-permute-start = (f32[16,4096]{1,0:T(8,128)S(1)}, f32[16,4096]{1,0:T(8,128)S(1)}, u32[]{:S(2)}, u32[]{:S(2)}) collective-permute-start(f32[16,4096]{1,0:T(8,128)S(1)} %copy.111), channel_id=1, source_target_pairs={{0,16},{16,32},{32,48},{48,64},{64,80},{80,96},{96,112},{1,17},{17... | collective-permute-start | bytes 786440 | tf_op jit(solution)/shard_map/while/body/eval_jaxpr/ppermute | solution.py:12
where the time goes:
time: 391 us; the launch traced here: 387 us
  matrix products  176 us (45%)
  other arithmetic  137 us (35%)
  starting transfers between devices  39.2 us (10%)
  local copies, waits for them, and re-layouts  32.3 us (8%)
    add x64, other arithmetic, add_source(): sum_imag = sum_imag + (lag_real * src_imag + lag_imag * src_real)  132 us
    dot_general x8, matrix products, spectrum(): imag_part = -jnp.einsum('cnt,tf->cnf', rows, sine, precision=highest)  77.7 us
    dot_general x8, matrix products, spectrum(): real_part = jnp.einsum('cnt,tf->cnf', rows, cosine, precision=highest)  77.6 us
    ppermute x8, starting transfers between devices, from_behind(): lax.ppermute(value, axis, [(source, source + steps) for source in range(f...  26 us
    all_to_all x1, starting transfers between devices, body(): lax.all_to_all(featured, 'chan', split_axis=1, concat_axis=2, tiled=True)  13.2 us
    slice x1, local copies, waits for them, and re-layouts, body(): filter_spectra[:, :, 1, :]  11.4 us
    dot_general x1, matrix products, body(): jnp.einsum('cnf,tf->cnt', acc_real, cosine, precision=highest)  10.2 us
    dot_general x1, matrix products, body(): jnp.einsum('cnf,tf->cnt', acc_imag, sine, precision=highest)  10 us
  transfers between devices with their start and end apart: 9, of which 0 were waited for; matrix products, arithmetic and copies ran while one was open for 72% of the time, Pallas kernels for 0%

commit v1 on v0

v1 whole, which is shorter than its diff:
```python
import math

import jax
import jax.numpy as jnp
import numpy as np
from jax import lax
from jax.sharding import PartitionSpec as P

HIGH = lax.Precision.HIGH


def tables(sub, lags):
    freq = 2 * sub
    width = sub + 128
    s = np.arange(sub)[:, None]
    f = np.arange(width)[None, :]
    angle = 2 * np.pi * ((s * f) % freq) / freq
    keep = (f <= sub).astype(np.float64)
    weight = np.where((f == 0) | (f == sub), 1.0, 2.0) * keep / freq
    cos, sin = np.cos(angle), np.sin(angle)
    forward = np.concatenate([cos * keep, -sin * keep], axis=1)
    inverse = np.concatenate([(cos * weight).T, (-sin * weight).T], axis=0)
    turns = 2 * lags
    k = np.arange(turns)[:, None]
    p = np.arange(lags)[None, :]
    theta = 2 * np.pi * ((k * p) % turns) / turns
    c, sn = np.cos(theta), np.sin(theta)
    across = np.block([[c, sn], [-sn, c]])
    back = np.block([[c.T, -sn.T], [sn.T, c.T]]) / turns
    return [np.asarray(t, np.float32) for t in (forward, inverse, across, back)]


def body(projections, taps, filter_spectra, skip_gain):
    chan_count, seq_count = lax.axis_size("chan"), lax.axis_size("seq")
    count = chan_count * seq_count
    streams, channels, tokens = projections.shape
    mine = channels // count
    length = tokens * count
    lags = filter_spectra.shape[1]
    sub = filter_spectra.shape[3] // 2
    local = filter_spectra.shape[0]
    forward, inverse, across, back = (jnp.asarray(t) for t in tables(sub, lags))
    within = lax.axis_index("seq") * mine
    offset = lax.axis_index("chan") * local + within
    my_taps = lax.dynamic_slice_in_dim(taps, offset, mine, 1)
    my_gain = lax.dynamic_slice_in_dim(skip_gain, offset, mine, 0)
    my_filter = lax.dynamic_slice_in_dim(filter_spectra, within, mine, 0)

    sent = projections.reshape(streams, count, mine, tokens)
    got = lax.all_to_all(sent, ("chan", "seq"), 1, 1, tiled=True)
    got = got.reshape(streams, chan_count, seq_count, mine, tokens)
    rows = got.transpose(0, 3, 2, 1, 4).reshape(streams, mine, length).astype(jnp.float32)
    edge = taps.shape[2] - 1
    padded = jnp.pad(rows, ((0, 0), (0, 0), (edge, 0)))
    features = sum(
        my_taps[:, :, i : i + 1] * padded[:, :, edge - i : edge - i + length] for i in range(edge + 1)
    )
    query, key, value = features[0], features[1], features[2]
    product = key * value

    g = my_filter[:, :, :, : sub + 1]
    mirror = jnp.concatenate([my_filter[:, :, :, :1], my_filter[:, :, :, sub:][:, :, :, ::-1]], axis=3)
    flip = jnp.array([0.5, -0.5], jnp.float32)[:, None]
    herm = jnp.pad(0.5 * g + flip * mirror, ((0, 0), (0, 0), (0, 0), (0, 127)))
    herm = herm.transpose(0, 2, 1, 3).reshape(mine, 2 * lags, sub + 128)
    ghat = jnp.einsum("kp,cpf->ckf", across, herm, precision=HIGH)

    spec = jnp.einsum("cps,sf->cpf", product.reshape(mine, lags, sub), forward, precision=HIGH)
    spec = spec.reshape(mine, lags, 2, sub + 128).transpose(0, 2, 1, 3).reshape(mine, 2 * lags, sub + 128)
    xhat = jnp.einsum("kp,cpf->ckf", across, spec, precision=HIGH)
    turns = 2 * lags
    gr, gi, xr, xi = ghat[:, :turns], ghat[:, turns:], xhat[:, :turns], xhat[:, turns:]
    yhat = jnp.concatenate([gr * xr - gi * xi, gr * xi + gi * xr], axis=1)
    mixed = jnp.einsum("nk,ckf->cnf", back, yhat, precision=HIGH)
    mixed = mixed.reshape(mine, 2, lags, sub + 128).transpose(0, 2, 1, 3).reshape(mine, lags, 2 * sub + 256)
    long_part = jnp.einsum("cnf,fs->cns", mixed, inverse, precision=HIGH).reshape(mine, length)
    out = (query * (long_part + my_gain[:, None] * product)).astype(jnp.bfloat16)
    out = out.reshape(mine, seq_count, length // seq_count).transpose(1, 0, 2)
    out = lax.all_to_all(out, "seq", 0, 0, tiled=True)
    return out.reshape(local, length // seq_count)


def solution(mesh):
    placed = (P(None, None, ("seq", "chan")), P(), P("chan", None, None, None), P())
    return jax.shard_map(
        body, mesh=mesh, in_specs=placed, out_specs=P("chan", "seq"), check_vma=False
    )
```

time: 391 us -> 44.4 us (0.11)
  matrix products: 176 us -> 4.27 us
  other arithmetic: 137 us -> 4.18 us
  starting transfers between devices: 39.2 us -> 11.1 us
  local copies, waits for them, and re-layouts: 32.3 us -> 11.1 us
  blocking collectives: 0 us -> 8.97 us
  waiting for transfers between devices: 0.02 us -> 4.13 us
    dot_general x18 -> x5, matrix products: 176 us -> 4.27 us  [the longest x1 1.5 us: body(): jnp.einsum('cps,sf->cpf', product.reshape(mine, lags, sub), forward, prec...]
    add x65 -> x2, other arithmetic: 135 us -> 3.54 us  [the longest x1 1.84 us: body(): herm = jnp.pad(0.5 * g + flip * mirror, ((0, 0), (0, 0), (0, 0), (0, 127)))]
    ppermute x8 -> x0, starting transfers between devices: 26 us -> none  [from_behind(): lax.ppermute(value, axis, [(source, source + steps) for source in range(f...]
    slice x4 -> x6, local copies, waits for them, and re-layouts: 12.6 us -> 3.17 us  [the longest x4 1.17 us: body(): my_taps[:, :, i:i + 1] * padded[:, :, edge - i:edge - i + length]]
    all_to_all x0 -> x1, blocking collectives: none -> 8.97 us  [body(): out = lax.all_to_all(out, 'seq', 0, 0, tiled=True)]
    squeeze x1 -> x0, local copies, waits for them, and re-layouts: 5.55 us -> none  [body(): filter_spectra[:, :, 1, :]]
    concatenate x2 -> x0, local copies, waits for them, and re-layouts: 5.53 us -> none  [the longest x1 2.79 us: body(): jnp.concatenate([lead_zeros, filter_spectra[:, :, 1, :]], axis=1)]
    all_to_all x1, waiting for transfers between devices: 0.01 us -> 4.13 us  [body(): got = lax.all_to_all(sent, ('chan', 'seq'), 1, 1, tiled=True)]
  transfers between devices with their start and end apart: 9 -> 1, of which waited for: 0 -> 1; matrix products, arithmetic and copies ran while one was open for 72% -> 18% of each run, Pallas kernels for 0% -> 0%
where the time goes in v1:
time: 44.4 us; the launch traced here: 44 us
  local copies, waits for them, and re-layouts  11.1 us (25%)
  starting transfers between devices  11.1 us (25%)
  blocking collectives  8.97 us (20%)
  matrix products  4.27 us (10%)
  other arithmetic  4.18 us (9%)
  waiting for transfers between devices  4.13 us (9%)
    all_to_all x1, starting transfers between devices, body(): got = lax.all_to_all(sent, ('chan', 'seq'), 1, 1, tiled=True)  11.1 us
    all_to_all x1, blocking collectives, body(): out = lax.all_to_all(out, 'seq', 0, 0, tiled=True)  8.97 us
    all_to_all x1, waiting for transfers between devices, body(): got = lax.all_to_all(sent, ('chan', 'seq'), 1, 1, tiled=True)  4.13 us
    reshape x2, local copies, waits for them, and re-layouts, body(): sent = projections.reshape(streams, count, mine, tokens)  2.19 us
    add x1, other arithmetic, body(): herm = jnp.pad(0.5 * g + flip * mirror, ((0, 0), (0, 0), (0, 0), (0, 127)))  1.84 us
    add x1, other arithmetic, body(): sum((my_taps[:, :, i:i + 1] * padded[:, :, edge - i:edge - i + length] fo...  1.7 us
    dot_general x1, matrix products, body(): jnp.einsum('cps,sf->cpf', product.reshape(mine, lags, sub), forward, prec...  1.5 us
    rev x1, local copies, waits for them, and re-layouts, body(): my_filter[:, :, :, sub:][:, :, :, ::-1]  1.34 us
  transfers between devices with their start and end apart: 1, of which 1 were waited for; matrix products, arithmetic and copies ran while one was open for 18% of the time, Pallas kernels for 0%

profile of v1, /device:TPU:0, one launch (start us, length us, event | category | flops | bytes accessed | tf_op | source)
XLA Modules:
  0.0 44.0 jit_solution(17891019297608231758)
XLA Ops:
  0.0 0.0 copy-start.4
  0.0 0.0 copy-start.5
  0.0 1.2 %reshape.46 = bf16[3,128,2,256]{3,2,1,0:T(2,128)(2,1)S(1)} reshape(bf16[3,256,256]{2,1,0:T(8,128)(2,1)} %param.9) | data formatting | bytes 786432 | tf_op jit(solution)/shard_map/reshape | solution.py:49
  1.2 1.0 %copy.56 = bf16[3,128,2,256]{3,2,0,1:T(2,128)(2,1)} copy(bf16[3,128,2,256]{3,2,1,0:T(2,128)(2,1)S(1)} %reshape.46) | data formatting | bytes 786432 | tf_op jit(solution)/shard_map/reshape | solution.py:49
  2.2 11.1 %all-to-all-start = ((bf16[3,128,2,256]{3,2,0,1:T(2,128)(2,1)}), bf16[3,128,2,256]{3,2,0,1:T(2,128)(2,1)S(1)}, u32[]{:S(2)}, u32[]{:S(2)}) async-start(bf16[3,128,2,256]{3,2,0,1:T(2,128)(2,1)} %copy.56), calls=%async_computation | async-start | bytes 786432 | tf_op jit(solution)/shard_map/all_to_all | solution.py:50
  13.4 0.9 %constant_dynamic-slice_fusion = f32[2,64,2,1]{3,2,1,0:T(2,128)S(1)} fusion(f32[16,64,2,1024]{3,2,1,0:T(2,128)} %param.11, s32[]{:T(128)S(6)} %select_n.8), kind=kLoop, calls=%fused_computation.23 | loop fusion | bytes 2052 | tf_op jit(solution)/shard_map/slice | solution.py:62
  14.3 1.1 %constant_dynamic-slice_fusion.3 = f32[2,64,2,512]{3,2,1,0:T(2,128)S(1)} fusion(f32[16,64,2,1024]{3,2,1,0:T(2,128)} %param.11, s32[]{:T(128)S(6)} %select_n.8, s32[]{:T(128)S(6)} %add.40), kind=kLoop, calls=%fused_computation.26 | loop fusion | bytes 1048584 | tf_op jit(solution)/shard_map/slice | solution.py:62
  15.4 0.0 copy-start.2
  15.4 1.3 %rev.3 = f32[2,64,2,512]{3,2,1,0:T(2,128)S(1)} reverse(f32[2,64,2,512]{3,2,1,0:T(2,128)S(1)} %constant_dynamic-slice_fusion.3), dimensions={3} | reverse | bytes 1048576 | tf_op jit(solution)/shard_map/rev | solution.py:62
  16.7 0.0 copy-done.5
  16.7 0.1 dynamic_slice.11
  16.8 0.0 copy-done.4
  16.8 1.8 %fusion.4 = f32[2,64,2,513]{3,2,1,0:T(2,128)S(1)} fusion(f32[16,64,2,1024]{3,2,1,0:T(2,128)} %param.11, s32[]{:T(128)S(6)} %select_n.8, f32[2,64,2,512]{3,2,1,0:T(2,128)S(1)} %rev.3, f32[2,64,2,1]{3,2,1,0:T(2,128)S(1)} %constant_dynamic-slice_fusion, f32[2]{0:T(128)S(1)} %copy-done.4), kind=kLoop, calls=%fused_computation.9 | loop fusion | flops 525312 | bytes 1575948 | tf_op jit(solution)/shard_map/add | solution.py:64
  18.7 0.9 %constant_dynamic-slice_fusion.2 = (f32[3,2,1]{1,2,0:T(1,128)S(1)}, f32[3,2,1]{1,2,0:T(1,128)S(1)}, f32[3,2,1]{1,2,0:T(1,128)S(1)}) fusion(f32[3,256,3]{1,2,0:T(4,128)} %param.10, s32[]{:T(128)S(6)} %select_n.7, s32[]{:T(128)S(6)} %add.38, s32[]{:T(128)S(6)} %add.39), kind=kLoop, calls=%fused_computation.25 | loop fusion | bytes 156 | tf_op jit(solution)/shard_map/slice | solution.py:56
  19.6 0.1 copy.54
  19.7 0.1 copy.55
  19.8 0.1 copy.58
  19.8 0.1 copy.59
  19.9 0.1 copy.60
  20.0 0.1 copy.61
  20.1 0.2 pad.9
  20.4 0.5 %reshape.53 = f32[2,128,640]{2,1,0:T(8,128)S(1)} reshape(f32[2,64,2,640]{3,2,1,0:T(2,128)S(1)} %pad.9) | data formatting | bytes 1310720 | tf_op jit(solution)/shard_map/kp,cpf->ckf/dot_general | solution.py:66
  20.8 0.0 copy-done.2
  20.8 0.7 %convolution_bitcast_fusion.1 = f32[2,256,640]{2,1,0:T(8,128)S(1)} fusion(f32[2,128,640]{2,1,0:T(8,128)S(1)} %reshape.53, f32[256,128,1]{1,0,2:T(8,128)S(1)} %copy-done.2), kind=kOutput, calls=%fused_computation.1 | convolution fusion | flops 251658240 | bytes 2097152 | tf_op jit(solution)/shard_map/kp,cpf->ckf/dot_general | solution.py:66
  21.5 4.1 %all-to-all-done = bf16[3,128,2,256]{3,2,0,1:T(2,128)(2,1)S(1)} async-done(((bf16[3,128,2,256]{3,2,0,1:T(2,128)(2,1)}), bf16[3,128,2,256]{3,2,0,1:T(2,128)(2,1)S(1)}, u32[]{:S(2)}, u32[]{:S(2)}) %all-to-all-start) | async-done | bytes 393248 | tf_op jit(solution)/shard_map/all_to_all | solution.py:50
  25.6 0.1 copy.84
  25.8 0.5 %reshape.59 = f32[3,2,32768]{2,1,0:T(2,128)S(1)} reshape(f32[3,2,8,16,256]{4,3,2,1,0:T(8,128)S(1)} %bitcast.63) | data formatting | bytes 1572864 | tf_op jit(solution)/shard_map/convert_element_type | solution.py:52
  26.3 0.0 copy-start.1
  26.3 1.7 %multiply_add_fusion = f32[3,2,32768]{2,1,0:T(2,128)S(1)} fusion(f32[3,2,32768]{2,1,0:T(2,128)S(1)} %reshape.59, f32[3,2]{1,0:T(4,128)S(1)} %copy.61, f32[3,2]{1,0:T(4,128)S(1)} %copy.59, f32[3,2]{1,0:T(4,128)S(1)} %copy.55), kind=kLoop, calls=%fused_computation.7 | loop fusion | flops 983040 | bytes 1572936 | tf_op jit(solution)/shard_map/add | solution.py:55
  28.0 0.1 fusion.13
  28.2 0.0 copy-done.1
  28.2 1.5 %fusion.9 = f32[2,64,2,640]{3,1,2,0:T(8,128)S(1)} fusion(f32[2,640,512,1]{2,1,0,3:T(8,128)S(1)} %copy-done.1, f32[1,2,64,512]{3,1,2,0:T(2,128)S(1)} %bitcast.67), kind=kOutput, calls=%fused_computation.19 | convolution fusion | flops 503316480 | bytes 3538944 | tf_op jit(solution)/shard_map/cps,sf->cpf/dot_general | solution.py:68
  29.7 0.5 %copy.62 = f32[2,64,2,640]{3,0,2,1:T(2,128)S(1)} copy(f32[2,64,2,640]{3,1,2,0:T(8,128)S(1)} %fusion.9) | data formatting | bytes 1310720 | tf_op jit(solution)/shard_map/cps,sf->cpf/dot_general | solution.py:68
  30.2 0.0 copy-start.3
  30.2 0.7 %convolution_bitcast_fusion = f32[2,256,640]{2,1,0:T(8,128)S(1)} fusion(f32[256,128,1]{1,0,2:T(8,128)S(1)} %copy-done.2, f32[2,128,640]{2,0,1:T(2,128)S(1)} %bitcast.66), kind=kOutput, calls=%fused_computation | convolution fusion | flops 251658240 | bytes 2097152 | tf_op jit(solution)/shard_map/kp,cpf->ckf/dot_general | solution.py:70
  30.9 0.2 multiply_subtract_fusion
  31.1 0.0 copy-start
  31.1 0.0 copy-done.3
  31.1 0.5 %fusion = f32[2,640,128]{1,2,0:T(8,128)S(1)} fusion(f32[128,256,1]{1,0,2:T(8,128)S(1)} %copy-done.3, f32[2,128,640]{2,1,0:T(8,128)S(1)} %get-tuple-element.6, f32[2,128,640]{2,1,0:T(8,128)S(1)} %get-tuple-element.5), kind=kOutput, calls=%fused_computation.2 | convolution fusion | flops 251985920 | bytes 2097152 | tf_op jit(solution)/shard_map/nk,ckf->cnf/dot_general | solution.py:74
  31.7 1.2 %copy-done = f32[1280,512,1]{1,0,2:T(8,128)S(1)} copy-done((f32[1280,512,1]{1,0,2:T(8,128)S(1)}, f32[1280,512,1]{1,0,2:T(8,128)}, u32[]{:S(2)}) %copy-start) | copy-done | bytes 2621464
  32.8 1.0 %fusion.14 = f32[2,64,512]{2,1,0:T(8,128)S(1)} fusion(f32[2,64,1280]{2,1,0:T(8,128)S(1)} %bitcast.64, f32[1280,512,1]{1,0,2:T(8,128)S(1)} %copy-done), kind=kOutput, calls=%fused_computation.30 | convolution fusion | flops 503316480 | bytes 3538944 | tf_op jit(solution)/shard_map/cnf,fs->cns/dot_general | solution.py:76
  33.8 0.1 reshape.51
  33.9 0.3 fusion.11
  34.2 0.1 copy.65
  34.3 9.0 %all_to_all.10 = bf16[8,2,4096]{2,1,0:T(2,128)(2,1)S(1)} all-to-all(bf16[8,2,4096]{2,1,0:T(2,128)(2,1)S(1)} %copy.65), channel_id=1, replica_groups=mesh['seq'=8,'chan'=16] {'seq'}, dimensions={0} | all-to-all | bytes 262144 | tf_op jit(solution)/shard_map/all_to_all | solution.py:79
  43.3 0.7 %reshape.52 = bf16[16,4096]{1,0:T(8,128)(2,1)} reshape(bf16[8,2,4096]{2,1,0:T(2,128)(2,1)S(1)} %all_to_all.10) | data formatting | bytes 262144 | tf_op jit(solution)/shard_map/reshape | solution.py:80
  (1 shorter events, 0.0 us)
Async XLA Ops:
  0.0 16.8 %copy-start.4 = (f32[2]{0:T(128)S(1)}, f32[2]{0:T(128)}, u32[]{:S(2)}) copy-start(f32[2]{0:T(128)} %constant.35.clone) | copy-start | bytes 28
  0.0 16.7 %copy-start.5 = (f32[256]{0:T(256)S(1)}, f32[256]{0:T(256)}, u32[]{:S(2)}) copy-start(f32[256]{0:T(256)} %param.12) | copy-start | bytes 3076
  2.2 23.4 %all-to-all-start = ((bf16[3,128,2,256]{3,2,0,1:T(2,128)(2,1)}), bf16[3,128,2,256]{3,2,0,1:T(2,128)(2,1)S(1)}, u32[]{:S(2)}, u32[]{:S(2)}) async-start(bf16[3,128,2,256]{3,2,0,1:T(2,128)(2,1)} %copy.56), calls=%async_computation | async-start | bytes 786432 | tf_op jit(solution)/shard_map/all_to_all | solution.py:50
  15.4 5.5 %copy-start.2 = (f32[256,128,1]{1,0,2:T(8,128)S(1)}, f32[256,128,1]{1,0,2:T(8,128)}, u32[]{:S(2)}) copy-start(f32[256,128,1]{1,0,2:T(8,128)} %constant.45) | copy-start | bytes 393220
  26.3 1.9 %copy-start.1 = (f32[2,640,512,1]{2,1,0,3:T(8,128)S(1)}, f32[2,640,512,1]{2,1,0,3:T(8,128)}, u32[]{:S(2)}) copy-start(f32[2,640,512,1]{2,1,0,3:T(8,128)} %constant.46) | copy-start | bytes 7864324
  30.2 0.9 %copy-start.3 = (f32[128,256,1]{1,0,2:T(8,128)S(1)}, f32[128,256,1]{1,0,2:T(8,128)}, u32[]{:S(2)}) copy-start(f32[128,256,1]{1,0,2:T(8,128)} %constant.47) | copy-start | bytes 393220
  31.1 1.8 %copy-start = (f32[1280,512,1]{1,0,2:T(8,128)S(1)}, f32[1280,512,1]{1,0,2:T(8,128)}, u32[]{:S(2)}) copy-start(f32[1280,512,1]{1,0,2:T(8,128)} %constant.48) | copy-start | bytes 7864324

commit v2 on v1

v2 whole, which is shorter than its diff:
```python
import math

import jax
import jax.numpy as jnp
import numpy as np
from jax import lax
from jax.experimental import pallas as pl
from jax.experimental.pallas import tpu as pltpu
from jax.sharding import PartitionSpec as P

F32, BF16 = jnp.float32, jnp.bfloat16


def halves(x):
    high = x.astype(BF16)
    return high, (x - high.astype(F32)).astype(BF16)


def table(x):
    high = np.asarray(x, np.float32).astype(BF16)
    low = (np.asarray(x, np.float64) - high.astype(np.float64)).astype(BF16)
    return jnp.asarray(high), jnp.asarray(low)


def dot(a, b):
    return jnp.dot(a, b, preferred_element_type=F32)


def dot_t(a, b):
    return lax.dot_general(a, b, (((1,), (1,)), ((), ())), preferred_element_type=F32)


def block_table(sub, width):
    freq = 2 * sub
    s = np.arange(sub)[:, None]
    f = np.arange(width)[None, :]
    angle = 2 * np.pi * ((s * f) % freq) / freq
    keep = f <= sub
    return np.concatenate([np.cos(angle) * keep, -np.sin(angle) * keep], axis=1)


def lag_tables(lags):
    turns = 2 * lags
    k = np.arange(turns)[:, None]
    p = np.arange(lags)[None, :]
    theta = 2 * np.pi * ((k * p) % turns) / turns
    c, sn = np.cos(theta), np.sin(theta)
    across = np.block([[c, sn], [-sn, c]])
    woven = across.reshape(2 * turns, 2, lags).transpose(0, 2, 1).reshape(2 * turns, 2 * lags)
    back = np.block([[c.T, -sn.T], [sn.T, c.T]]) / turns
    return across, woven, back


def filter_kernel(g_ref, high_ref, low_ref, out_ref):
    mine, rows, freq = g_ref.shape
    tiles = freq // 128
    lane = lax.broadcasted_iota(jnp.int32, (rows, 128), 1)
    row = lax.broadcasted_iota(jnp.int32, (rows, 128), 0)
    sign = jnp.where(row % 2 == 0, 1.0, -1.0).astype(F32)
    behind = (128 - lane) % 128
    for r in range(mine):
        parts = []
        for t in range(tiles // 2):
            here = g_ref[r, :, t * 128 : t * 128 + 128]
            far = g_ref[r, :, freq - t * 128 - 128 : freq - t * 128]
            edge = (tiles - t) % tiles
            first = g_ref[r, :, edge * 128 : edge * 128 + 128]
            mirror = jnp.where(lane == 0, first, jnp.take_along_axis(far, behind, axis=1))
            scale = jnp.where((lane == 0) & (t == 0), 0.5 / freq, 1.0 / freq).astype(F32)
            parts.append((here + sign * mirror) * scale)
        half = g_ref[r, :, freq // 2 : freq // 2 + 128]
        parts.append(jnp.where(lane == 0, (half + sign * half) * (0.5 / freq), 0.0))
        high, low = halves(jnp.concatenate(parts, axis=1))
        out_ref[r] = dot(high_ref[...], high) + dot(high_ref[...], low) + dot(low_ref[...], high)


def shifted(pair, by, lane, first_row):
    turned = [pltpu.roll(x, by, 1) for x in pair]
    down = jnp.where(first_row, 0.0, pltpu.roll(turned[1][:, :128], 1, 0))
    inner = [down, turned[0][:, :128]]
    return [
        jnp.concatenate([jnp.where(lane < by, inner[h], turned[h][:, :128]), turned[h][:, 128:]], axis=1)
        for h in range(2)
    ]


def main_kernel(scal_ref, rows_ref, ghat_ref, wh_ref, wl_ref, ah_ref, al_ref, bh_ref, bl_ref, out_ref):
    streams, mine, two, lags, chunk = rows_ref.shape
    width = ghat_ref.shape[2]
    turns = 2 * lags
    lane = lax.broadcasted_iota(jnp.int32, (lags, 128), 1)
    first_row = lax.broadcasted_iota(jnp.int32, (lags, 128), 0) == 0
    features = []
    for g in range(streams):
        per = []
        for r in range(mine):
            pair = [rows_ref[g, r, h] for h in range(2)]
            one, two_back = shifted(pair, 1, lane, first_row), shifted(pair, 2, lane, first_row)
            t = [scal_ref[(g * mine + r) * 3 + i] for i in range(3)]
            per.append(
                jnp.concatenate([t[0] * pair[h] + t[1] * one[h] + t[2] * two_back[h] for h in range(2)], axis=1)
            )
        features.append(per)
    product = [features[1][r] * features[2][r] for r in range(mine)]
    high, low = halves(jnp.concatenate(product, axis=0))
    spec = dot(high, wh_ref[...]) + dot(low, wh_ref[...]) + dot(high, wl_ref[...])
    mixed = []
    for r in range(mine):
        mine_spec = spec[r * lags : (r + 1) * lags]
        zh, zl = halves(jnp.concatenate([mine_spec[:, :width], mine_spec[:, width:]], axis=0))
        xhat = dot(ah_ref[...], zh) + dot(ah_ref[...], zl) + dot(al_ref[...], zh)
        xr, xi = xhat[:turns], xhat[turns:]
        gr, gi = ghat_ref[r, :turns], ghat_ref[r, turns:]
        yh, yl = halves(jnp.concatenate([gr * xr - gi * xi, gr * xi + gi * xr], axis=0))
        m = dot(bh_ref[...], yh) + dot(bh_ref[...], yl) + dot(bl_ref[...], yh)
        mixed.append(jnp.concatenate([m[:lags], m[lags:]], axis=1))
    mh, ml = halves(jnp.concatenate(mixed, axis=0))
    long_part = dot_t(mh, wh_ref[...]) + dot_t(ml, wh_ref[...]) + dot_t(mh, wl_ref[...])
    for r in range(mine):
        gain = scal_ref[streams * mine * 3 + r]
        out_ref[r] = features[0][r] * (long_part[r * lags : (r + 1) * lags] + gain * product[r])


def body(projections, taps, filter_spectra, skip_gain):
    chan_count, seq_count = lax.axis_size("chan"), lax.axis_size("seq")
    count = chan_count * seq_count
    streams, channels, tokens = projections.shape
    mine = channels // count
    length = tokens * count
    lags = filter_spectra.shape[1]
    freq = filter_spectra.shape[3]
    sub = freq // 2
    width = sub + 128
    local = filter_spectra.shape[0]
    wh, wl = table(block_table(sub, width))
    across, woven, back = lag_tables(lags)
    ah, al = table(across)
    vh, vl = table(woven)
    bh, bl = table(back)
    within = lax.axis_index("seq") * mine
    offset = lax.axis_index("chan") * local + within
    my_taps = lax.dynamic_slice_in_dim(taps, offset, mine, 1)
    my_gain = lax.dynamic_slice_in_dim(skip_gain, offset, mine, 0)
    scalars = jnp.concatenate([my_taps.reshape(-1), my_gain])
    my_filter = lax.dynamic_slice_in_dim(filter_spectra, within, mine, 0)
    vmem, smem = pl.BlockSpec(memory_space=pltpu.VMEM), pl.BlockSpec(memory_space=pltpu.SMEM)

    got = lax.all_to_all(projections, ("chan", "seq"), 1, 1, tiled=True)
    ghat = pl.pallas_call(
        filter_kernel,
        out_shape=jax.ShapeDtypeStruct((mine, 4 * lags, width), F32),
        in_specs=[vmem] * 3,
        out_specs=vmem,
        compiler_params=pltpu.CompilerParams(vmem_limit_bytes=16 << 20),
        cost_estimate=pl.CostEstimate(flops=3 * 2 * mine * 4 * lags * 2 * lags * width, bytes_accessed=4 << 20, transcendentals=0),
    )(my_filter.reshape(mine, 2 * lags, freq), vh, vl)
    per = sub // tokens
    got = got.reshape(streams, chan_count // per, per, seq_count, mine, tokens)
    rows = got.transpose(0, 4, 2, 3, 1, 5).reshape(streams, mine, per, lags, tokens).astype(F32)
    out = pl.pallas_call(
        main_kernel,
        out_shape=jax.ShapeDtypeStruct((mine, lags, sub), F32),
        in_specs=[smem] + [vmem] * 8,
        out_specs=vmem,
        compiler_params=pltpu.CompilerParams(vmem_limit_bytes=24 << 20),
        cost_estimate=pl.CostEstimate(flops=1 << 30, bytes_accessed=8 << 20, transcendentals=0),
    )(scalars, rows, ghat, wh, wl, ah, al, bh, bl)
    out = out.astype(BF16).reshape(mine, seq_count, length // seq_count).transpose(1, 0, 2)
    out = lax.all_to_all(out, "seq", 0, 0, tiled=True)
    return out.reshape(local, length // seq_count)


def solution(mesh):
    placed = (P(None, None, ("seq", "chan")), P(), P("chan", None, None, None), P())
    return jax.shard_map(
        body, mesh=mesh, in_specs=placed, out_specs=P("chan", "seq"), check_vma=False
    )
```

time: 44.4 us -> 43.2 us (0.973)
  waiting for transfers between devices: 4.13 us -> 10.2 us
  Pallas kernels: 0 us -> 5.11 us
  matrix products: 4.27 us -> 0 us
  other arithmetic: 4.18 us -> 0.1 us
  local copies, waits for them, and re-layouts: 11.1 us -> 7.2 us
    all_to_all x1, waiting for transfers between devices: 4.13 us -> 10.2 us  [body(): got = lax.all_to_all(projections, ('chan', 'seq'), 1, 1, tiled=True)]
    pallas_call x0 -> x2, Pallas kernels: none -> 5.11 us  [the longest x1 4.31 us: body(): pl.pallas_call(main_kernel, out_shape=jax.ShapeDtypeStruct((mine, lags, s...]
    dot_general x5 -> x0, matrix products: 4.27 us -> none  [the longest x1 1.5 us: body(): jnp.einsum('cps,sf->cpf', product.reshape(mine, lags, sub), forward, prec...]
    add x2 -> x0, other arithmetic: 3.54 us -> none  [the longest x1 1.84 us: body(): herm = jnp.pad(0.5 * g + flip * mirror, ((0, 0), (0, 0), (0, 0), (0, 127)))]
    slice x6 -> x0, local copies, waits for them, and re-layouts: 3.17 us -> none  [the longest x4 1.17 us: body(): my_taps[:, :, i:i + 1] * padded[:, :, edge - i:edge - i + length]]
    unnamed x12 -> x21, local copies, waits for them, and re-layouts: 1.22 us -> 3.62 us
    dynamic_slice x0 -> x3, local copies, waits for them, and re-layouts: none -> 1.48 us  [the longest x1 1.3 us: body(): my_filter = lax.dynamic_slice_in_dim(filter_spectra, within, mine, 0)]
    rev x1 -> x0, local copies, waits for them, and re-layouts: 1.34 us -> none  [body(): my_filter[:, :, :, sub:][:, :, :, ::-1]]
  transfers between devices with their start and end apart: 1 -> 1, of which waited for: 1 -> 1; matrix products, arithmetic and copies ran while one was open for 18% -> 6% of each run, Pallas kernels for 0% -> 2%
where the time goes in v2:
time: 43.2 us; the launch traced here: 42.9 us
  starting transfers between devices  11.1 us (26%)
  waiting for transfers between devices  10.2 us (24%)
  blocking collectives  8.97 us (21%)
  local copies, waits for them, and re-layouts  7.2 us (17%)
  Pallas kernels  5.11 us (12%)
    all_to_all x1, starting transfers between devices, body(): got = lax.all_to_all(projections, ('chan', 'seq'), 1, 1, tiled=True)  11.1 us
    all_to_all x1, waiting for transfers between devices, body(): got = lax.all_to_all(projections, ('chan', 'seq'), 1, 1, tiled=True)  10.2 us
    all_to_all x1, blocking collectives, body(): out = lax.all_to_all(out, 'seq', 0, 0, tiled=True)  8.97 us
    pallas_call x1, Pallas kernels, body(): pl.pallas_call(main_kernel, out_shape=jax.ShapeDtypeStruct((mine, lags, s...  4.31 us
    unnamed x21, local copies, waits for them, and re-layouts  3.62 us
    dynamic_slice x1, local copies, waits for them, and re-layouts, body(): my_filter = lax.dynamic_slice_in_dim(filter_spectra, within, mine, 0)  1.3 us
  transfers between devices with their start and end apart: 1, of which 1 were waited for; matrix products, arithmetic and copies ran while one was open for 6% of the time, Pallas kernels for 2%

profile of v2, /device:TPU:0, one launch (start us, length us, event | category | flops | bytes accessed | tf_op | source)
XLA Modules:
  0.0 42.9 jit_solution(16703043159708187924)
XLA Ops:
  0.0 0.0 copy-start
  0.0 0.0 copy-start.9
  0.0 2.1 %copy.17 = bf16[3,256,256]{2,0,1:T(4,128)(2,1)} copy(bf16[3,256,256]{2,1,0:T(8,128)(2,1)} %param.12) | data formatting | bytes 786432 | tf_op args[0]
  2.2 11.1 %all-to-all-start = ((bf16[3,256,256]{2,0,1:T(4,128)(2,1)}), bf16[3,256,256]{2,0,1:T(4,128)(2,1)S(1)}, u32[]{:S(2)}, u32[]{:S(2)}) async-start(bf16[3,256,256]{2,0,1:T(4,128)(2,1)} %copy.17), calls=%async_computation | async-start | bytes 1048576 | tf_op jit(solution)/shard_map/all_to_all | solution.py:148
  13.3 0.0 copy-done
  13.3 0.1 constant_dynamic-slice_fusion.1
  13.4 0.1 copy.16
  13.5 0.1 reshape.18
  13.6 0.0 copy-done.9
  13.6 0.1 dynamic_slice.10
  13.7 1.3 %constant_dynamic-slice_fusion = f32[2,64,2,1024]{3,2,1,0:T(2,128)S(1)} fusion(f32[16,64,2,1024]{3,2,1,0:T(2,128)} %param.14, s32[]{:T(128)S(6)} %select_n.8), kind=kLoop, calls=%fused_computation.3 | loop fusion | bytes 2097156 | tf_op jit(solution)/shard_map/dynamic_slice | solution.py:145
  15.0 0.0 copy-start.7
  15.0 0.0 copy-start.8
  15.0 0.7 %reshape.19.g_ref = f32[2,128,1024]{2,1,0:T(8,128)S(1)} reshape(f32[2,64,2,1024]{3,2,1,0:T(2,128)S(1)} %constant_dynamic-slice_fusion) | data formatting | bytes 2097152 | tf_op jit(solution)/shard_map/reshape | solution.py:156
  15.7 0.1 copy-done.7
  15.8 0.0 copy-done.8
  15.8 0.0 copy-start.3
  15.9 0.0 copy-start.4
  15.9 0.0 copy-start.5
  15.9 0.0 copy-start.6
  15.9 0.8 %shard_map.118.ghat_ref = f32[2,256,640]{2,1,0:T(8,128)S(1)} custom-call(f32[2,128,1024]{2,1,0:T(8,128)S(1)} %reshape.19.g_ref, bf16[256,128]{1,0:T(8,128)(2,1)S(1)} %copy-done.7, bf16[256,128]{1,0:T(8,128)(2,1)S(1)} %copy-done.8), custom_call_target="tpu_custom_call" | custom-call | flops 251658240 | bytes 4194304 | tf_op jit(solution)/shard_map/pallas_call | solution.py:149
  16.7 0.0 copy-start.1
  16.7 0.1 pad_maximum_fusion.scal_ref
  16.8 10.2 %all-to-all-done = bf16[3,256,256]{2,0,1:T(4,128)(2,1)S(1)} async-done(((bf16[3,256,256]{2,0,1:T(4,128)(2,1)}), bf16[3,256,256]{2,0,1:T(4,128)(2,1)S(1)}, u32[]{:S(2)}, u32[]{:S(2)}) %all-to-all-start) | async-done | bytes 393248 | tf_op jit(solution)/shard_map/all_to_all | solution.py:148
  27.0 0.3 copy.22
  27.3 0.0 copy-done.3
  27.3 0.0 copy-done.4
  27.3 0.0 copy-done.5
  27.3 0.0 copy-done.6
  27.3 0.0 copy-done.1
  27.3 0.0 copy-start.2
  27.3 1.3 %copy-done.2 = bf16[512,1280]{1,0:T(8,128)(2,1)S(1)} copy-done((bf16[512,1280]{1,0:T(8,128)(2,1)S(1)}, bf16[512,1280]{1,0:T(8,128)(2,1)}, u32[]{:S(2)}) %copy-start.2) | copy-done | bytes 1310744
  28.7 4.3 %shard_map.119 = f32[2,64,512]{2,1,0:T(8,128)S(1)} custom-call(f32[20]{0:T(128)S(1)} %pad_maximum_fusion.scal_ref, f32[3,2,2,64,256]{4,3,2,1,0:T(8,128)S(1)} %bitcast.10, f32[2,256,640]{2,1,0:T(8,128)S(1)} %shard_map.118.ghat_ref, bf16[512,1280]{1,0:T(8,128)(2,1)S(1)} %copy-done.1, bf16[512,1280]{1,0:T(8,128)(2,1)S(1)} %copy-done.2, ...), custom_call_target="tpu_custom_call" | custom-call | flops 1073741824 | bytes 8388608 | tf_op jit(solution)/shard_map/pallas_call | solution.py:160
  33.0 0.1 reshape.20
  33.1 0.1 copy.23
  33.2 9.0 %all_to_all.10 = bf16[8,2,4096]{2,1,0:T(2,128)(2,1)S(1)} all-to-all(bf16[8,2,4096]{2,1,0:T(2,128)(2,1)S(1)} %bitcast.12), channel_id=1, replica_groups=mesh['seq'=8,'chan'=16] {'seq'}, dimensions={0} | all-to-all | bytes 262144 | tf_op jit(solution)/shard_map/all_to_all | solution.py:169
  42.2 0.7 %reshape.21 = bf16[16,4096]{1,0:T(8,128)(2,1)} reshape(bf16[8,2,4096]{2,1,0:T(2,128)(2,1)S(1)} %all_to_all.10) | data formatting | bytes 262144 | tf_op jit(solution)/shard_map/reshape | solution.py:170
  (1 shorter events, 0.0 us)
Async XLA Ops:
  0.0 13.3 %copy-start = (f32[3,256,3]{1,2,0:T(4,128)S(1)}, f32[3,256,3]{1,2,0:T(4,128)}, u32[]{:S(2)}) copy-start(f32[3,256,3]{1,2,0:T(4,128)} %param.13) | copy-start | bytes 27652
  0.0 13.6 %copy-start.9 = (f32[256]{0:T(256)S(1)}, f32[256]{0:T(256)}, u32[]{:S(2)}) copy-start(f32[256]{0:T(256)} %param.15) | copy-start | bytes 3076
  2.2 24.8 %all-to-all-start = ((bf16[3,256,256]{2,0,1:T(4,128)(2,1)}), bf16[3,256,256]{2,0,1:T(4,128)(2,1)S(1)}, u32[]{:S(2)}, u32[]{:S(2)}) async-start(bf16[3,256,256]{2,0,1:T(4,128)(2,1)} %copy.17), calls=%async_computation | async-start | bytes 1048576 | tf_op jit(solution)/shard_map/all_to_all | solution.py:148
  15.0 0.8 %copy-start.7 = (bf16[256,128]{1,0:T(8,128)(2,1)S(1)}, bf16[256,128]{1,0:T(8,128)(2,1)}, u32[]{:S(2)}) copy-start(bf16[256,128]{1,0:T(8,128)(2,1)} %constant.37.clone.high_ref) | copy-start | bytes 196612
  15.0 0.9 %copy-start.8 = (bf16[256,128]{1,0:T(8,128)(2,1)S(1)}, bf16[256,128]{1,0:T(8,128)(2,1)}, u32[]{:S(2)}) copy-start(bf16[256,128]{1,0:T(8,128)(2,1)} %constant.38.clone.low_ref) | copy-start | bytes 196612
  15.8 11.4 %copy-start.3 = (bf16[256,128]{1,0:T(8,128)(2,1)S(1)}, bf16[256,128]{1,0:T(8,128)(2,1)}, u32[]{:S(2)}) copy-start(bf16[256,128]{1,0:T(8,128)(2,1)} %constant.35.clone.ah_ref) | copy-start | bytes 196612
  15.9 11.4 %copy-start.4 = (bf16[256,128]{1,0:T(8,128)(2,1)S(1)}, bf16[256,128]{1,0:T(8,128)(2,1)}, u32[]{:S(2)}) copy-start(bf16[256,128]{1,0:T(8,128)(2,1)} %constant.36.clone.al_ref) | copy-start | bytes 196612
  15.9 11.5 %copy-start.5 = (bf16[128,256]{1,0:T(8,128)(2,1)S(1)}, bf16[128,256]{1,0:T(8,128)(2,1)}, u32[]{:S(2)}) copy-start(bf16[128,256]{1,0:T(8,128)(2,1)} %constant.39.clone.bh_ref) | copy-start | bytes 196612
  15.9 11.5 %copy-start.6 = (bf16[128,256]{1,0:T(8,128)(2,1)S(1)}, bf16[128,256]{1,0:T(8,128)(2,1)}, u32[]{:S(2)}) copy-start(bf16[128,256]{1,0:T(8,128)(2,1)} %constant.40.clone.bl_ref) | copy-start | bytes 196612
  16.7 10.7 %copy-start.1 = (bf16[512,1280]{1,0:T(8,128)(2,1)S(1)}, bf16[512,1280]{1,0:T(8,128)(2,1)}, u32[]{:S(2)}) copy-start(bf16[512,1280]{1,0:T(8,128)(2,1)} %constant.33.clone.wh_ref) | copy-start | bytes 3932164
  27.3 1.3 %copy-start.2 = (bf16[512,1280]{1,0:T(8,128)(2,1)S(1)}, bf16[512,1280]{1,0:T(8,128)(2,1)}, u32[]{:S(2)}) copy-start(bf16[512,1280]{1,0:T(8,128)(2,1)} %constant.34.clone.wl_ref) | copy-start | bytes 3932164

commit v3 on v2

v3 whole, which is shorter than its diff:
```python
import jax
import jax.numpy as jnp
import numpy as np
from jax import lax
from jax.experimental import pallas as pl
from jax.experimental.pallas import tpu as pltpu
from jax.sharding import PartitionSpec as P

F32, BF16 = jnp.float32, jnp.bfloat16


def halves(x):
    high = x.astype(BF16)
    return high, (x - high.astype(F32)).astype(BF16)


def table(x):
    high = np.asarray(x, np.float32).astype(BF16)
    low = (np.asarray(x, np.float64) - high.astype(np.float64)).astype(BF16)
    return high, low


def dot(a, b):
    return jnp.dot(a, b, preferred_element_type=F32)


def fixed(x):
    return pltpu.with_memory_space_constraint(jnp.asarray(x), pltpu.HBM)


def join(parts, axis):
    return jnp.concatenate(parts, axis=axis)


def block_tables(sub):
    freq = 2 * sub
    s = np.arange(sub)[:, None]
    f = np.arange(sub)[None, :]
    angle = 2 * np.pi * ((s * f) % freq) / freq
    imag = -np.sin(angle)
    imag[:, 0] = 1.0 - 2.0 * (np.arange(sub) % 2)
    forward = np.concatenate([np.cos(angle), imag], axis=1)
    return forward, np.ascontiguousarray(forward.T)


def lag_tables(lags, order):
    turns = 2 * lags
    k = np.arange(turns)[:, None]

    def turn(p):
        theta = 2 * np.pi * ((k * p[None, :]) % turns) / turns
        c, sn = np.cos(theta), np.sin(theta)
        return c, sn, np.block([[c, sn], [-sn, c]])

    woven = turn(np.arange(lags))[2]
    woven = woven.reshape(2 * turns, 2, lags).transpose(0, 2, 1).reshape(2 * turns, 2 * lags)
    c, sn, across = turn(order)
    back = np.block([[c.T, -sn.T], [sn.T, c.T]]) / turns
    return across, woven, back


def send_kernel(x_ref, out_ref, x_buf, out_buf, in_sem, out_sem):
    count, streams, mine, tokens = out_ref.shape
    reads = [pltpu.make_async_copy(x_ref.at[g], x_buf.at[g], in_sem.at[g]) for g in range(streams)]
    for read in reads:
        read.start()
    for g in range(streams):
        reads[g].wait()
        out_buf[:, g] = x_buf[g].reshape(count, mine, tokens)
    write = pltpu.make_async_copy(out_buf, out_ref, out_sem)
    write.start()
    write.wait()


def filter_kernel(g_hbm, taps_hbm, gain_hbm, lag_hbm, *refs):
    tables_hbm, out_ref, scal_ref, tables_ref = refs[:3], refs[3], refs[4], refs[5:8]
    g_ref, taps_ref, gain_ref, lag_ref, sems = refs[8:]
    mine, lags, two, freq = g_ref.shape
    local = g_hbm.shape[0]
    rows = lags * two
    tiles = freq // 128
    place = lax.axis_index("seq") * mine
    offset = lax.axis_index("chan") * local + place
    copies = [
        pltpu.make_async_copy(g_hbm.at[pl.ds(place, mine)], g_ref, sems.at[0]),
        pltpu.make_async_copy(lag_hbm, lag_ref, sems.at[1]),
        pltpu.make_async_copy(taps_hbm, taps_ref, sems.at[2]),
        pltpu.make_async_copy(gain_hbm, gain_ref, sems.at[3]),
    ]
    copies += [pltpu.make_async_copy(tables_hbm[k], tables_ref[k], sems.at[4 + k]) for k in range(3)]
    for copy in copies:
        copy.start()
    copies[3].wait()
    copies[2].wait()
    streams, edge_taps, channels = taps_ref.shape
    at = lax.broadcasted_iota(jnp.int32, (edge_taps, channels), 1)
    odd = lax.broadcasted_iota(jnp.int32, scal_ref.shape[1:], 0) % 2 == 1

    def pick(x, r):
        hit = lax.broadcasted_iota(jnp.int32, x.shape, 1) == offset + r
        return jnp.sum(jnp.where(hit, x, 0.0), axis=1, keepdims=True)

    for g in range(streams):
        even, second = (pick(taps_ref[g], r) for r in range(2))
        for i in range(edge_taps):
            scal_ref[g * edge_taps + i] = jnp.where(odd, second[i : i + 1], even[i : i + 1])
    even, second = (pick(gain_ref[...], r) for r in range(2))
    scal_ref[streams * edge_taps] = jnp.where(odd, second, even)

    lane = lax.broadcasted_iota(jnp.int32, (rows, 128), 1)
    row = lax.broadcasted_iota(jnp.int32, (rows, 128), 0)
    sign = jnp.where(row % 2 == 0, 1.0, -1.0).astype(F32)
    behind = (128 - lane) % 128
    copies[1].wait()
    copies[0].wait()
    wide = 2 * rows
    gh, gl = lag_ref[:wide], lag_ref[wide:]
    for r in range(mine):
        g = g_ref[r].reshape(rows, freq)
        parts = []
        for t in range(tiles // 2):
            here = g[:, t * 128 : t * 128 + 128]
            far = g[:, freq - t * 128 - 128 : freq - t * 128]
            edge = (tiles - t) % tiles
            first = g[:, edge * 128 : edge * 128 + 128]
            mirror = jnp.where(lane == 0, first, jnp.take_along_axis(far, behind, axis=1))
            scale = jnp.where((lane == 0) & (t == 0), 0.5 / freq, 1.0 / freq).astype(F32)
            parts.append((here + sign * mirror) * scale)
        half = g[:, freq // 2 : freq // 2 + 128]
        parts.append(jnp.where(lane == 0, (half + sign * half) * (0.5 / freq), 0.0))
        high, low = halves(join(parts, 1))
        out_ref[r] = dot(gh, high) + dot(gh, low) + dot(gl, high)
    for copy in copies[4:]:
        copy.wait()


def shifted(pair, by, inner, lane, first):
    turned = [pltpu.roll(x, by, 1).astype(F32) for x in pair]
    heads = [x[:, :128] for x in turned]
    count = heads[1].shape[0]
    step = count // inner
    last = jnp.where(first, 0.0, pltpu.roll(heads[1][count - step :], 2, 0))
    before = [join([last, heads[1][: count - step]], 0), heads[0]]
    return [join([jnp.where(lane < by, before[h], heads[h]), turned[h][:, 128:]], 1) for h in range(2)]


def main_kernel(got_ref, ghat_ref, scal_ref, w_ref, v_ref, lag_ref, out_ref):
    count, streams, mine, chunk = got_ref.shape
    sub = w_ref.shape[1]
    turns = ghat_ref.shape[1] // 2
    lags = turns // 2
    per = sub // chunk
    steps = out_ref.shape[0]
    inner = lags // steps
    rows = lags * mine
    lane = lax.broadcasted_iota(jnp.int32, (rows, 128), 1)
    first = lax.broadcasted_iota(jnp.int32, (steps * mine, 128), 0) < mine

    def spread(k):
        return jnp.tile(scal_ref[k], (rows // scal_ref.shape[1], 1))

    features = []
    for g in range(streams):
        x = got_ref[:, g].reshape(inner, per, steps * mine, chunk)
        pair = [x[:, h].reshape(rows, chunk) for h in range(per)]
        one, far = (shifted(pair, by, inner, lane, first) for by in (1, 2))
        t = [spread(3 * g + i) for i in range(3)]
        features.append(join([t[0] * pair[h].astype(F32) + t[1] * one[h] + t[2] * far[h] for h in range(per)], 1))
    query, key, value = features
    product = key * value
    high, low = halves(product)
    spec = dot(high, w_ref[0]) + dot(low, w_ref[0]) + dot(high, w_ref[1])
    spec = spec.reshape(lags, mine, 2 * sub)
    parts = []
    for r in range(mine):
        own = spec[:, r]
        parts.append(join([own[:, :sub], own[:, sub:]], 0))
    zh, zl = halves(join(parts, 1))
    wide = 2 * turns
    ahh, bhl, bh = lag_ref[:wide], lag_ref[wide : 2 * wide], lag_ref[2 * wide : 2 * wide + turns]
    al = lag_ref[2 * wide + turns :]
    al = join([al[:, :turns], al[:, turns:]], 0)
    xhat = dot(ahh, join([zh, zl], 0)) + dot(al, zh)
    parts, tails = [], []
    for r in range(mine):
        xr, xi = (xhat[k : k + turns, r * sub : (r + 1) * sub] for k in (0, turns))
        gr, gi = (ghat_ref[r, k : k + turns, :] for k in (0, turns))
        for real, imag, out, w in ((gr[:, :sub], gi[:, :sub], parts, sub), (gr[:, sub:], gi[:, sub:], tails, 128)):
            ur, ui = xr[:, :w], xi[:, :w]
            out.append(join([real * ur - imag * ui, real * ui + imag * ur], 0))
    yh, yl = halves(join(parts + tails, 1))
    both = dot(bhl, yh)
    mixed = both[:turns] + both[turns:] + dot(bh, yl)
    zero = lax.broadcasted_iota(jnp.int32, (lags, 128), 1) == 0
    parts = []
    for r in range(mine):
        real = mixed[:lags, r * sub : (r + 1) * sub]
        imag = mixed[lags:, r * sub : (r + 1) * sub]
        tail = mixed[lags:, mine * sub + r * 128 : mine * sub + (r + 1) * 128]
        parts.append(join([real, jnp.where(zero, tail, imag[:, :128]), imag[:, 128:]], 1))
    mh, ml = halves(join(parts, 0))
    long_part = dot(mh, v_ref[0]) + dot(ml, v_ref[0]) + dot(mh, v_ref[1])
    long_part = jnp.stack([long_part[r * lags : (r + 1) * lags] for r in range(mine)], axis=1).reshape(rows, sub)
    gain = jnp.tile(spread(3 * streams), (1, per))
    gated = (query * (long_part + gain * product)).astype(BF16).reshape(inner, steps, mine, sub)
    for b in range(inner):
        out_ref[:, :, b * sub : (b + 1) * sub] = gated[b]


def body(projections, taps, filter_spectra, skip_gain):
    chan_count, seq_count = lax.axis_size("chan"), lax.axis_size("seq")
    count = chan_count * seq_count
    streams, channels, tokens = projections.shape
    mine = channels // count
    length = tokens * count
    lags = filter_spectra.shape[1]
    freq = filter_spectra.shape[3]
    sub = freq // 2
    width = sub + 128
    local = filter_spectra.shape[0]
    per = sub // tokens
    inner = chan_count // per
    forward, inverse = block_tables(sub)
    order = np.arange(lags).reshape(seq_count, inner).T.reshape(-1)
    across, woven, back = lag_tables(lags, order)
    w, v = np.stack(table(forward)), np.stack(table(inverse))
    ah, al = table(across)
    bh, bl = table(back)
    woven = np.concatenate(table(woven), axis=0)
    al = np.concatenate([al[: 2 * lags], al[2 * lags :]], axis=1)
    lag = np.concatenate([np.concatenate([ah, ah], axis=1), bh, bl, bh, al], axis=0)
    vmem, hbm = pl.BlockSpec(memory_space=pltpu.VMEM), pl.BlockSpec(memory_space=pltpu.HBM)
    dma = pltpu.SemaphoreType.DMA

    sent = pl.pallas_call(
        send_kernel,
        out_shape=jax.ShapeDtypeStruct((count, streams, mine, tokens), BF16),
        in_specs=[hbm],
        out_specs=hbm,
        scratch_shapes=[
            pltpu.VMEM((streams, channels, tokens), BF16),
            pltpu.VMEM((count, streams, mine, tokens), BF16),
            dma((streams,)),
            dma,
        ],
        compiler_params=pltpu.CompilerParams(vmem_limit_bytes=8 << 20),
    )(fixed(projections))
    got = lax.all_to_all(sent, ("chan", "seq"), 0, 0, tiled=True)
    tables = w, v, lag
    ghat, scalars, *ready = pl.pallas_call(
        filter_kernel,
        out_shape=[
            jax.ShapeDtypeStruct((mine, 4 * lags, width), F32),
            jax.ShapeDtypeStruct((streams * 3 + 1, 8, tokens), F32),
        ]
        + [jax.ShapeDtypeStruct(t.shape, BF16) for t in tables],
        in_specs=[hbm] * 7,
        out_specs=[vmem] * 5,
        scratch_shapes=[
            pltpu.VMEM((mine,) + filter_spectra.shape[1:], F32),
            pltpu.VMEM((streams, taps.shape[2], channels), F32),
            pltpu.VMEM((1, channels), F32),
            pltpu.VMEM(woven.shape, BF16),
            dma((7,)),
        ],
        compiler_params=pltpu.CompilerParams(vmem_limit_bytes=12 << 20),
        cost_estimate=pl.CostEstimate(flops=1 << 28, bytes_accessed=4 << 20, transcendentals=0),
    )(*map(fixed, (filter_spectra, taps.transpose(0, 2, 1), skip_gain.reshape(1, channels), woven, *tables)))
    out = pl.pallas_call(
        main_kernel,
        out_shape=jax.ShapeDtypeStruct((seq_count, mine, length // seq_count), BF16),
        in_specs=[vmem] * 6,
        out_specs=vmem,
        compiler_params=pltpu.CompilerParams(vmem_limit_bytes=24 << 20),
        cost_estimate=pl.CostEstimate(flops=1 << 30, bytes_accessed=8 << 20, transcendentals=0),
    )(got, ghat, scalars, *ready)
    out = lax.all_to_all(out, "seq", 0, 0, tiled=True)
    return out.reshape(local, length // seq_count)


def solution(mesh):
    placed = (P(None, None, ("seq", "chan")), P(), P("chan", None, None, None), P())
    return jax.shard_map(
        body, mesh=mesh, in_specs=placed, out_specs=P("chan", "seq"), check_vma=False
    )
```

time: 43.2 us -> 40.8 us (0.944)
  waiting for transfers between devices: 10.2 us -> 7.16 us
  Pallas kernels: 5.11 us -> 7.15 us
  local copies, waits for them, and re-layouts: 7.2 us -> 6.02 us
    all_to_all x1, waiting for transfers between devices: 10.2 us -> 7.16 us  [body(): got = lax.all_to_all(sent, ('chan', 'seq'), 0, 0, tiled=True)]
    pallas_call x2 -> x3, Pallas kernels: 5.11 us -> 7.15 us  [the longest x1 2.71 us: body(): pl.pallas_call(filter_kernel, out_shape=[jax.ShapeDtypeStruct((mine, 4 *...]
    unnamed x21 -> x8, local copies, waits for them, and re-layouts: 3.62 us -> 5.31 us
    dynamic_slice x4 -> x0, local copies, waits for them, and re-layouts: 1.56 us -> none  [the longest x1 1.3 us: body(): my_filter = lax.dynamic_slice_in_dim(filter_spectra, within, mine, 0)]
    reshape x4 -> x0, local copies, waits for them, and re-layouts: 1.01 us -> none  [the longest x1 0.72 us: body(): my_filter.reshape(mine, 2 * lags, freq)]
  transfers between devices with their start and end apart: 1 -> 1, of which waited for: 1 -> 1; matrix products, arithmetic and copies ran while one was open for 6% -> 0% of each run, Pallas kernels for 2% -> 7%
where the time goes in v3:
time: 40.8 us; the launch traced here: 40.5 us
  starting transfers between devices  11.1 us (27%)
  blocking collectives  8.97 us (22%)
  waiting for transfers between devices  7.16 us (18%)
  Pallas kernels  7.15 us (18%)
  local copies, waits for them, and re-layouts  6.02 us (15%)
    all_to_all x1, starting transfers between devices, body(): got = lax.all_to_all(sent, ('chan', 'seq'), 0, 0, tiled=True)  11.1 us
    all_to_all x1, blocking collectives, body(): out = lax.all_to_all(out, 'seq', 0, 0, tiled=True)  8.97 us
    all_to_all x1, waiting for transfers between devices, body(): got = lax.all_to_all(sent, ('chan', 'seq'), 0, 0, tiled=True)  7.16 us
    unnamed x8, local copies, waits for them, and re-layouts  5.31 us
    pallas_call x1, Pallas kernels, body(): pl.pallas_call(filter_kernel, out_shape=[jax.ShapeDtypeStruct((mine, 4 *...  2.71 us
    pallas_call x1, Pallas kernels, body(): pl.pallas_call(main_kernel, out_shape=jax.ShapeDtypeStruct((seq_count, mi...  2.58 us
    pallas_call x1, Pallas kernels, body(): pl.pallas_call(send_kernel, out_shape=jax.ShapeDtypeStruct((count, stream...  1.86 us
  transfers between devices with their start and end apart: 1, of which 1 were waited for; matrix products, arithmetic and copies ran while one was open for 0% of the time, Pallas kernels for 7%

profile of v3, /device:TPU:0, one launch (start us, length us, event | category | flops | bytes accessed | tf_op | source)
XLA Modules:
  0.0 40.5 jit_solution(12917671404228701444)
XLA Ops:
  0.0 1.9 %shard_map.82 = bf16[128,3,2,256]{3,2,1,0:T(2,128)(2,1)} custom-call(bf16[3,256,256]{2,1,0:T(8,128)(2,1)} %x_ref.1), custom_call_target="tpu_custom_call" | custom-call | tf_op jit(solution)/shard_map/pallas_call | solution.py:235
  1.9 11.1 %all-to-all-start = ((bf16[128,3,2,256]{3,2,1,0:T(2,128)(2,1)}), bf16[128,3,2,256]{3,2,1,0:T(2,128)(2,1)S(1)}, u32[]{:S(2)}, u32[]{:S(2)}) async-start(bf16[128,3,2,256]{3,2,1,0:T(2,128)(2,1)} %shard_map.82), calls=%async_computation | async-start | bytes 786432 | tf_op jit(solution)/shard_map/all_to_all | solution.py:248
  13.0 2.7 %shard_map.83 = (f32[2,256,640]{2,1,0:T(8,128)S(1)}, f32[10,8,256]{2,1,0:T(8,128)S(1)}, bf16[2,512,1024]{2,1,0:T(8,128)(2,1)S(1)}, bf16[2,1024,512]{2,1,0:T(8,128)(2,1)S(1)}, bf16[768,256]{1,0:T(8,128)(2,1)S(1)}) custom-call(f32[16,64,2,1024]{3,2,1,0:T(2,128)} %g_hbm.1, f32[3,3,256]{2,1,0:T(4,128)} %bitcast.2, f32[1,256]{1,0:T(1,128)} %bitcast.3, ...), custom_call_target="tpu_custom_call" | custom-call | flops 268435456 | bytes 4194304 | tf_op jit(solution)/shard_map/pallas_call | solution.py:250
  15.7 0.0 copy-start
  15.8 1.3 %copy-done = bf16[2,1024,512]{2,1,0:T(8,128)(2,1)} copy-done((bf16[2,1024,512]{2,1,0:T(8,128)(2,1)}, bf16[2,1024,512]{2,1,0:T(8,128)(2,1)S(1)}, u32[]{:S(2)}) %copy-start) | copy-done | bytes 2097176
  17.1 0.0 copy-start.2
  17.1 1.1 %copy-done.2 = f32[2,256,640]{2,1,0:T(8,128)} copy-done((f32[2,256,640]{2,1,0:T(8,128)}, f32[2,256,640]{2,1,0:T(8,128)S(1)}, u32[]{:S(2)}) %copy-start.2) | copy-done | bytes 1310744
  18.2 7.2 %all-to-all-done.got_ref = bf16[128,3,2,256]{3,2,1,0:T(2,128)(2,1)S(1)} async-done(((bf16[128,3,2,256]{3,2,1,0:T(2,128)(2,1)}), bf16[128,3,2,256]{3,2,1,0:T(2,128)(2,1)S(1)}, u32[]{:S(2)}, u32[]{:S(2)}) %all-to-all-start) | async-done | bytes 393248 | tf_op jit(solution)/shard_map/all_to_all | solution.py:248
  25.3 0.0 copy-start.1
  25.3 1.6 %copy-done.1 = bf16[2,1024,512]{2,1,0:T(8,128)(2,1)S(1)} copy-done((bf16[2,1024,512]{2,1,0:T(8,128)(2,1)S(1)}, bf16[2,1024,512]{2,1,0:T(8,128)(2,1)}, u32[]{:S(2)}) %copy-start.1) | copy-done | bytes 2097176
  26.9 0.0 copy-start.3
  26.9 1.3 %copy-done.3 = f32[2,256,640]{2,1,0:T(8,128)S(1)} copy-done((f32[2,256,640]{2,1,0:T(8,128)S(1)}, f32[2,256,640]{2,1,0:T(8,128)}, u32[]{:S(2)}) %copy-start.3) | copy-done | bytes 1310744
  28.2 2.6 %shard_map.84 = bf16[8,2,4096]{2,1,0:T(2,128)(2,1)S(1)} custom-call(bf16[128,3,2,256]{3,2,1,0:T(2,128)(2,1)S(1)} %all-to-all-done.got_ref, f32[2,256,640]{2,1,0:T(8,128)S(1)} %copy-done.3, f32[10,8,256]{2,1,0:T(8,128)S(1)} %get-tuple-element.11.scal_ref, bf16[2,512,1024]{2,1,0:T(8,128)(2,1)S(1)} %get-tuple-element.12.w_ref, ...), custom_call_target="tpu_custom_call" | custom-call | flops 1073741824 | bytes 8388608 | tf_op jit(solution)/shard_map/pallas_call | solution.py:269
  30.8 9.0 %all_to_all.10 = bf16[8,2,4096]{2,1,0:T(2,128)(2,1)S(1)} all-to-all(bf16[8,2,4096]{2,1,0:T(2,128)(2,1)S(1)} %shard_map.84), channel_id=1, replica_groups=mesh['seq'=8,'chan'=16] {'seq'}, dimensions={0} | all-to-all | bytes 262144 | tf_op jit(solution)/shard_map/all_to_all | solution.py:277
  39.8 0.7 %reshape.7 = bf16[16,4096]{1,0:T(8,128)(2,1)} reshape(bf16[8,2,4096]{2,1,0:T(2,128)(2,1)S(1)} %all_to_all.10) | data formatting | bytes 262144 | tf_op jit(solution)/shard_map/reshape | solution.py:278
Async XLA Ops:
  1.9 23.4 %all-to-all-start = ((bf16[128,3,2,256]{3,2,1,0:T(2,128)(2,1)}), bf16[128,3,2,256]{3,2,1,0:T(2,128)(2,1)S(1)}, u32[]{:S(2)}, u32[]{:S(2)}) async-start(bf16[128,3,2,256]{3,2,1,0:T(2,128)(2,1)} %shard_map.82), calls=%async_computation | async-start | bytes 786432 | tf_op jit(solution)/shard_map/all_to_all | solution.py:248
  15.7 1.4 %copy-start = (bf16[2,1024,512]{2,1,0:T(8,128)(2,1)}, bf16[2,1024,512]{2,1,0:T(8,128)(2,1)S(1)}, u32[]{:S(2)}) copy-start(bf16[2,1024,512]{2,1,0:T(8,128)(2,1)S(1)} %get-tuple-element.13.v_ref) | copy-start | bytes 6291460
  17.1 1.1 %copy-start.2 = (f32[2,256,640]{2,1,0:T(8,128)}, f32[2,256,640]{2,1,0:T(8,128)S(1)}, u32[]{:S(2)}) copy-start(f32[2,256,640]{2,1,0:T(8,128)S(1)} %get-tuple-element.10.ghat_ref) | copy-start | bytes 3932164
  25.3 1.6 %copy-start.1 = (bf16[2,1024,512]{2,1,0:T(8,128)(2,1)S(1)}, bf16[2,1024,512]{2,1,0:T(8,128)(2,1)}, u32[]{:S(2)}) copy-start(bf16[2,1024,512]{2,1,0:T(8,128)(2,1)} %copy-done) | copy-start | bytes 6291460
  26.9 1.3 %copy-start.3 = (f32[2,256,640]{2,1,0:T(8,128)S(1)}, f32[2,256,640]{2,1,0:T(8,128)}, u32[]{:S(2)}) copy-start(f32[2,256,640]{2,1,0:T(8,128)} %copy-done.2) | copy-start | bytes 3932164

commit v4 on v3

--- a/solution.py
+++ b/solution.py
@@ -73,8 +73,8 @@
 
 
 def filter_kernel(g_hbm, taps_hbm, gain_hbm, lag_hbm, *refs):
-    tables_hbm, out_ref, scal_ref, tables_ref = refs[:3], refs[3], refs[4], refs[5:8]
-    g_ref, taps_ref, gain_ref, lag_ref, sems = refs[8:]
+    tables_hbm, out_ref, scal_ref, tables_ref = refs[:2], refs[2], refs[3], refs[4:6]
+    g_ref, taps_ref, gain_ref, lag_ref, sems = refs[6:]
     mine, lags, two, freq = g_ref.shape
     local = g_hbm.shape[0]
     rows = lags * two
@@ -87,7 +87,7 @@
         pltpu.make_async_copy(taps_hbm, taps_ref, sems.at[2]),
         pltpu.make_async_copy(gain_hbm, gain_ref, sems.at[3]),
     ]
-    copies += [pltpu.make_async_copy(tables_hbm[k], tables_ref[k], sems.at[4 + k]) for k in range(3)]
+    copies += [pltpu.make_async_copy(tables_hbm[k], tables_ref[k], sems.at[4 + k]) for k in range(2)]
     for copy in copies:
         copy.start()
     copies[3].wait()
@@ -144,15 +144,19 @@
     return [join([jnp.where(lane < by, before[h], heads[h]), turned[h][:, 128:]], 1) for h in range(2)]
 
 
-def main_kernel(got_ref, ghat_ref, scal_ref, w_ref, v_ref, lag_ref, out_ref):
+def main_kernel(got_ref, ghat_ref, scal_ref, w_ref, lag_ref, low_hbm, v_hbm, out_ref, low_ref, v_ref, sems):
     count, streams, mine, chunk = got_ref.shape
-    sub = w_ref.shape[1]
+    sub = w_ref.shape[0]
     turns = ghat_ref.shape[1] // 2
     lags = turns // 2
     per = sub // chunk
     steps = out_ref.shape[0]
     inner = lags // steps
     rows = lags * mine
+    copies = [pltpu.make_async_copy(low_hbm, low_ref, sems.at[0])]
+    copies += [pltpu.make_async_copy(v_hbm.at[k], v_ref.at[k], sems.at[1 + k]) for k in range(2)]
+    for copy in copies:
+        copy.start()
     lane = lax.broadcasted_iota(jnp.int32, (rows, 128), 1)
     first = lax.broadcasted_iota(jnp.int32, (steps * mine, 128), 0) < mine
 
@@ -169,7 +173,9 @@
     query, key, value = features
     product = key * value
     high, low = halves(product)
-    spec = dot(high, w_ref[0]) + dot(low, w_ref[0]) + dot(high, w_ref[1])
+    spec = dot(high, w_ref[...]) + dot(low, w_ref[...])
+    copies[0].wait()
+    spec = spec + dot(high, low_ref[...])
     spec = spec.reshape(lags, mine, 2 * sub)
     parts = []
     for r in range(mine):
@@ -199,6 +205,8 @@
         tail = mixed[lags:, mine * sub + r * 128 : mine * sub + (r + 1) * 128]
         parts.append(join([real, jnp.where(zero, tail, imag[:, :128]), imag[:, 128:]], 1))
     mh, ml = halves(join(parts, 0))
+    copies[1].wait()
+    copies[2].wait()
     long_part = dot(mh, v_ref[0]) + dot(ml, v_ref[0]) + dot(mh, v_ref[1])
     long_part = jnp.stack([long_part[r * lags : (r + 1) * lags] for r in range(mine)], axis=1).reshape(rows, sub)
     gain = jnp.tile(spread(3 * streams), (1, per))
@@ -223,7 +231,8 @@
     forward, inverse = block_tables(sub)
     order = np.arange(lags).reshape(seq_count, inner).T.reshape(-1)
     across, woven, back = lag_tables(lags, order)
-    w, v = np.stack(table(forward)), np.stack(table(inverse))
+    wh, wl = table(forward)
+    v = np.stack(table(inverse))
     ah, al = table(across)
     bh, bl = table(back)
     woven = np.concatenate(table(woven), axis=0)
@@ -246,7 +255,7 @@
         compiler_params=pltpu.CompilerParams(vmem_limit_bytes=8 << 20),
     )(fixed(projections))
     got = lax.all_to_all(sent, ("chan", "seq"), 0, 0, tiled=True)
-    tables = w, v, lag
+    tables = wh, lag
     ghat, scalars, *ready = pl.pallas_call(
         filter_kernel,
         out_shape=[
@@ -254,14 +263,14 @@
             jax.ShapeDtypeStruct((streams * 3 + 1, 8, tokens), F32),
         ]
         + [jax.ShapeDtypeStruct(t.shape, BF16) for t in tables],
-        in_specs=[hbm] * 7,
-        out_specs=[vmem] * 5,
+        in_specs=[hbm] * 6,
+        out_specs=[vmem] * 4,
         scratch_shapes=[
             pltpu.VMEM((mine,) + filter_spectra.shape[1:], F32),
             pltpu.VMEM((streams, taps.shape[2], channels), F32),
             pltpu.VMEM((1, channels), F32),
             pltpu.VMEM(woven.shape, BF16),
-            dma((7,)),
+            dma((6,)),
         ],
         compiler_params=pltpu.CompilerParams(vmem_limit_bytes=12 << 20),
         cost_estimate=pl.CostEstimate(flops=1 << 28, bytes_accessed=4 << 20, transcendentals=0),
@@ -269,11 +278,12 @@
     out = pl.pallas_call(
         main_kernel,
         out_shape=jax.ShapeDtypeStruct((seq_count, mine, length // seq_count), BF16),
-        in_specs=[vmem] * 6,
+        in_specs=[vmem] * 5 + [hbm] * 2,
         out_specs=vmem,
+        scratch_shapes=[pltpu.VMEM(wl.shape, BF16), pltpu.VMEM(v.shape, BF16), dma((3,))],
         compiler_params=pltpu.CompilerParams(vmem_limit_bytes=24 << 20),
         cost_estimate=pl.CostEstimate(flops=1 << 30, bytes_accessed=8 << 20, transcendentals=0),
-    )(got, ghat, scalars, *ready)
+    )(got, ghat, scalars, *ready, fixed(wl), fixed(v))
     out = lax.all_to_all(out, "seq", 0, 0, tiled=True)
     return out.reshape(local, length // seq_count)
 

time: 40.8 us -> 38.6 us (0.946)
  local copies, waits for them, and re-layouts: 6.02 us -> 0.71 us
  waiting for transfers between devices: 7.16 us -> 9.9 us
  Pallas kernels: 7.15 us -> 7.6 us
    unnamed x8 -> x0, local copies, waits for them, and re-layouts: 5.31 us -> none
    all_to_all x1, waiting for transfers between devices: 7.16 us -> 9.9 us  [body(): got = lax.all_to_all(sent, ('chan', 'seq'), 0, 0, tiled=True)]
    pallas_call x1, Pallas kernels: 2.58 us -> 3.36 us  [body(): pl.pallas_call(main_kernel, out_shape=jax.ShapeDtypeStruct((seq_count, mi...]
  transfers between devices with their start and end apart: 1 -> 1, of which waited for: 1 -> 1; matrix products, arithmetic and copies ran while one was open for 0% -> 0% of each run, Pallas kernels for 7% -> 6%
where the time goes in v4:
time: 38.6 us; the launch traced here: 38.4 us
  starting transfers between devices  11.1 us (29%)
  waiting for transfers between devices  9.9 us (26%)
  blocking collectives  8.97 us (23%)
  Pallas kernels  7.6 us (20%)
  local copies, waits for them, and re-layouts  0.71 us (2%)
    all_to_all x1, starting transfers between devices, body(): got = lax.all_to_all(sent, ('chan', 'seq'), 0, 0, tiled=True)  11.1 us
    all_to_all x1, waiting for transfers between devices, body(): got = lax.all_to_all(sent, ('chan', 'seq'), 0, 0, tiled=True)  9.9 us
    all_to_all x1, blocking collectives, body(): out = lax.all_to_all(out, 'seq', 0, 0, tiled=True)  8.97 us
    pallas_call x1, Pallas kernels, body(): pl.pallas_call(main_kernel, out_shape=jax.ShapeDtypeStruct((seq_count, mi...  3.36 us
    pallas_call x1, Pallas kernels, body(): pl.pallas_call(filter_kernel, out_shape=[jax.ShapeDtypeStruct((mine, 4 *...  2.38 us
    pallas_call x1, Pallas kernels, body(): pl.pallas_call(send_kernel, out_shape=jax.ShapeDtypeStruct((count, stream...  1.86 us
  transfers between devices with their start and end apart: 1, of which 1 were waited for; matrix products, arithmetic and copies ran while one was open for 0% of the time, Pallas kernels for 6%

profile of v4, /device:TPU:0, one launch (start us, length us, event | category | flops | bytes accessed | tf_op | source)
XLA Modules:
  0.0 38.4 jit_solution(4929069647567144014)
XLA Ops:
  0.0 1.9 %shard_map.91 = bf16[128,3,2,256]{3,2,1,0:T(2,128)(2,1)} custom-call(bf16[3,256,256]{2,1,0:T(8,128)(2,1)} %x_ref.1), custom_call_target="tpu_custom_call" | custom-call | tf_op jit(solution)/shard_map/pallas_call | solution.py:244
  1.9 11.1 %all-to-all-start = ((bf16[128,3,2,256]{3,2,1,0:T(2,128)(2,1)}), bf16[128,3,2,256]{3,2,1,0:T(2,128)(2,1)S(1)}, u32[]{:S(2)}, u32[]{:S(2)}) async-start(bf16[128,3,2,256]{3,2,1,0:T(2,128)(2,1)} %shard_map.91), calls=%async_computation | async-start | bytes 786432 | tf_op jit(solution)/shard_map/all_to_all | solution.py:257
  13.0 2.4 %shard_map.92 = (f32[2,256,640]{2,1,0:T(8,128)S(1)}, f32[10,8,256]{2,1,0:T(8,128)S(1)}, bf16[512,1024]{1,0:T(8,128)(2,1)S(1)}, bf16[768,256]{1,0:T(8,128)(2,1)S(1)}) custom-call(f32[16,64,2,1024]{3,2,1,0:T(2,128)} %g_hbm.1, f32[3,3,256]{2,1,0:T(4,128)} %bitcast.2, f32[1,256]{1,0:T(1,128)} %bitcast.3, bf16[512,128]{1,0:T(8,128)(2,1)} %constant.10.clone.lag_hbm, ...), custom_call_target="tpu_custom_call" | custom-call | flops 268435456 | bytes 4194304 | tf_op jit(solution)/shard_map/pallas_call | solution.py:259
  15.4 9.9 %all-to-all-done.got_ref = bf16[128,3,2,256]{3,2,1,0:T(2,128)(2,1)S(1)} async-done(((bf16[128,3,2,256]{3,2,1,0:T(2,128)(2,1)}), bf16[128,3,2,256]{3,2,1,0:T(2,128)(2,1)S(1)}, u32[]{:S(2)}, u32[]{:S(2)}) %all-to-all-start) | async-done | bytes 393248 | tf_op jit(solution)/shard_map/all_to_all | solution.py:257
  25.3 3.4 %shard_map.93 = bf16[8,2,4096]{2,1,0:T(2,128)(2,1)S(1)} custom-call(bf16[128,3,2,256]{3,2,1,0:T(2,128)(2,1)S(1)} %all-to-all-done.got_ref, f32[2,256,640]{2,1,0:T(8,128)S(1)} %get-tuple-element.9.ghat_ref, f32[10,8,256]{2,1,0:T(8,128)S(1)} %get-tuple-element.10.scal_ref, bf16[512,1024]{1,0:T(8,128)(2,1)S(1)} %get-tuple-element.11.w_ref, ...), custom_call_target="tpu_custom_call" | custom-call | flops 1073741824 | bytes 8388608 | tf_op jit(solution)/shard_map/pallas_call | solution.py:278
  28.7 9.0 %all_to_all.10 = bf16[8,2,4096]{2,1,0:T(2,128)(2,1)S(1)} all-to-all(bf16[8,2,4096]{2,1,0:T(2,128)(2,1)S(1)} %shard_map.93), channel_id=1, replica_groups=mesh['seq'=8,'chan'=16] {'seq'}, dimensions={0} | all-to-all | bytes 262144 | tf_op jit(solution)/shard_map/all_to_all | solution.py:287
  37.7 0.7 %reshape.7 = bf16[16,4096]{1,0:T(8,128)(2,1)} reshape(bf16[8,2,4096]{2,1,0:T(2,128)(2,1)S(1)} %all_to_all.10) | data formatting | bytes 262144 | tf_op jit(solution)/shard_map/reshape | solution.py:288
Async XLA Ops:
  1.9 23.4 %all-to-all-start = ((bf16[128,3,2,256]{3,2,1,0:T(2,128)(2,1)}), bf16[128,3,2,256]{3,2,1,0:T(2,128)(2,1)S(1)}, u32[]{:S(2)}, u32[]{:S(2)}) async-start(bf16[128,3,2,256]{3,2,1,0:T(2,128)(2,1)} %shard_map.91), calls=%async_computation | async-start | bytes 786432 | tf_op jit(solution)/shard_map/all_to_all | solution.py:257

commit v5 on v4

--- a/solution.py
+++ b/solution.py
@@ -61,15 +61,22 @@
 
 def send_kernel(x_ref, out_ref, x_buf, out_buf, in_sem, out_sem):
     count, streams, mine, tokens = out_ref.shape
-    reads = [pltpu.make_async_copy(x_ref.at[g], x_buf.at[g], in_sem.at[g]) for g in range(streams)]
-    for read in reads:
-        read.start()
-    for g in range(streams):
-        reads[g].wait()
-        out_buf[:, g] = x_buf[g].reshape(count, mine, tokens)
-    write = pltpu.make_async_copy(out_buf, out_ref, out_sem)
-    write.start()
-    write.wait()
+    pieces = in_sem.shape[0]
+    share = count // pieces
+    reads, writes = [], []
+    for k in range(pieces):
+        rows, to = pl.ds(k * share * mine, share * mine), pl.ds(k * share, share)
+        reads.append(pltpu.make_async_copy(x_ref.at[:, rows], x_buf.at[:, rows], in_sem.at[k]))
+        writes.append(pltpu.make_async_copy(out_buf.at[to], out_ref.at[to], out_sem.at[k]))
+        reads[k].start()
+    for k in range(pieces):
+        reads[k].wait()
+        for g in range(streams):
+            part = x_buf[g, k * share * mine : (k + 1) * share * mine]
+            out_buf[k * share : (k + 1) * share, g] = part.reshape(share, mine, tokens)
+        writes[k].start()
+    for write in writes:
+        write.wait()
 
 
 def filter_kernel(g_hbm, taps_hbm, gain_hbm, lag_hbm, *refs):
@@ -94,18 +101,18 @@
     copies[2].wait()
     streams, edge_taps, channels = taps_ref.shape
     at = lax.broadcasted_iota(jnp.int32, (edge_taps, channels), 1)
-    odd = lax.broadcasted_iota(jnp.int32, scal_ref.shape[1:], 0) % 2 == 1
+    terms = scal_ref.shape[0] // mine
 
     def pick(x, r):
         hit = lax.broadcasted_iota(jnp.int32, x.shape, 1) == offset + r
         return jnp.sum(jnp.where(hit, x, 0.0), axis=1, keepdims=True)
 
-    for g in range(streams):
-        even, second = (pick(taps_ref[g], r) for r in range(2))
-        for i in range(edge_taps):
-            scal_ref[g * edge_taps + i] = jnp.where(odd, second[i : i + 1], even[i : i + 1])
-    even, second = (pick(gain_ref[...], r) for r in range(2))
-    scal_ref[streams * edge_taps] = jnp.where(odd, second, even)
+    for r in range(mine):
+        for g in range(streams):
+            own = pick(taps_ref[g], r)
+            for i in range(edge_taps):
+                scal_ref[r * terms + g * edge_taps + i] = jnp.broadcast_to(own[i : i + 1], scal_ref.shape[1:])
+        scal_ref[r * terms + terms - 1] = jnp.broadcast_to(pick(gain_ref[...], r), scal_ref.shape[1:])
 
     lane = lax.broadcasted_iota(jnp.int32, (rows, 128), 1)
     row = lax.broadcasted_iota(jnp.int32, (rows, 128), 0)
@@ -139,48 +146,45 @@
     heads = [x[:, :128] for x in turned]
     count = heads[1].shape[0]
     step = count // inner
-    last = jnp.where(first, 0.0, pltpu.roll(heads[1][count - step :], 2, 0))
+    last = jnp.where(first, 0.0, pltpu.roll(heads[1][count - step :], 1, 0))
     before = [join([last, heads[1][: count - step]], 0), heads[0]]
     return [join([jnp.where(lane < by, before[h], heads[h]), turned[h][:, 128:]], 1) for h in range(2)]
 
 
-def main_kernel(got_ref, ghat_ref, scal_ref, w_ref, lag_ref, low_hbm, v_hbm, out_ref, low_ref, v_ref, sems):
-    count, streams, mine, chunk = got_ref.shape
-    sub = w_ref.shape[0]
-    turns = ghat_ref.shape[1] // 2
-    lags = turns // 2
-    per = sub // chunk
-    steps = out_ref.shape[0]
-    inner = lags // steps
+def main_kernel(rows_ref, ghat_ref, scal_ref, w_ref, lag_ref, v_hbm, out_ref, v_ref, sems):
+    streams, mine, per, lags, chunk = rows_ref.shape
+    sub = per * chunk
+    turns = 2 * lags
     rows = lags * mine
-    copies = [pltpu.make_async_copy(low_hbm, low_ref, sems.at[0])]
-    copies += [pltpu.make_async_copy(v_hbm.at[k], v_ref.at[k], sems.at[1 + k]) for k in range(2)]
+    terms = scal_ref.shape[0] // mine
+    step = scal_ref.shape[1]
+    inner = lags // step
+    copies = [pltpu.make_async_copy(v_hbm.at[k], v_ref.at[k], sems.at[k]) for k in range(2)]
     for copy in copies:
         copy.start()
-    lane = lax.broadcasted_iota(jnp.int32, (rows, 128), 1)
-    first = lax.broadcasted_iota(jnp.int32, (steps * mine, 128), 0) < mine
-
-    def spread(k):
-        return jnp.tile(scal_ref[k], (rows // scal_ref.shape[1], 1))
-
-    features = []
-    for g in range(streams):
-        x = got_ref[:, g].reshape(inner, per, steps * mine, chunk)
-        pair = [x[:, h].reshape(rows, chunk) for h in range(per)]
+    lane = lax.broadcasted_iota(jnp.int32, (lags, 128), 1)
+    first = lax.broadcasted_iota(jnp.int32, (step, 128), 0) == 0
+
+    def spread(r, k, wide):
+        return jnp.tile(scal_ref[r * terms + k], (inner, wide // 128))
+
+    def feature(g, r):
+        pair = [rows_ref[g, r, h] for h in range(per)]
         one, far = (shifted(pair, by, inner, lane, first) for by in (1, 2))
-        t = [spread(3 * g + i) for i in range(3)]
-        features.append(join([t[0] * pair[h].astype(F32) + t[1] * one[h] + t[2] * far[h] for h in range(per)], 1))
-    query, key, value = features
-    product = key * value
-    high, low = halves(product)
-    spec = dot(high, w_ref[...]) + dot(low, w_ref[...])
-    copies[0].wait()
-    spec = spec + dot(high, low_ref[...])
-    spec = spec.reshape(lags, mine, 2 * sub)
-    parts = []
-    for r in range(mine):
-        own = spec[:, r]
-        parts.append(join([own[:, :sub], own[:, sub:]], 0))
+        t = [spread(r, 3 * g + i, chunk) for i in range(3)]
+        return [t[0] * pair[h].astype(F32) + t[1] * one[h] + t[2] * far[h] for h in range(per)]
+
+    query, key, value = ([feature(g, r) for r in range(mine)] for g in range(streams))
+    product = [[key[r][h] * value[r][h] for r in range(mine)] for h in range(per)]
+    high, low = halves(join([join(x, 0) for x in product], 0))
+    quarter = lax.broadcasted_iota(jnp.int32, (1, sub), 1) % 4
+    even = jnp.where(quarter == 0, 1.0, jnp.where(quarter == 2, -1.0, 0.0))
+    odd = jnp.where(quarter == 1, 1.0, jnp.where(quarter == 3, -1.0, 0.0))
+    spec = dot(high, w_ref[0]) + dot(low, w_ref[0]) + dot(high, w_ref[1])
+    ar, ai, br, bi = (spec[i : i + rows, k : k + sub] for i in (0, rows) for k in (0, sub))
+    real = ar + even * br + odd * bi
+    imag = ai + even * bi - odd * br
+    parts = [join([x[r * lags : (r + 1) * lags] for x in (real, imag)], 0) for r in range(mine)]
     zh, zl = halves(join(parts, 1))
     wide = 2 * turns
     ahh, bhl, bh = lag_ref[:wide], lag_ref[wide : 2 * wide], lag_ref[2 * wide : 2 * wide + turns]
@@ -205,14 +209,12 @@
         tail = mixed[lags:, mine * sub + r * 128 : mine * sub + (r + 1) * 128]
         parts.append(join([real, jnp.where(zero, tail, imag[:, :128]), imag[:, 128:]], 1))
     mh, ml = halves(join(parts, 0))
-    copies[1].wait()
-    copies[2].wait()
+    for copy in copies:
+        copy.wait()
     long_part = dot(mh, v_ref[0]) + dot(ml, v_ref[0]) + dot(mh, v_ref[1])
-    long_part = jnp.stack([long_part[r * lags : (r + 1) * lags] for r in range(mine)], axis=1).reshape(rows, sub)
-    gain = jnp.tile(spread(3 * streams), (1, per))
-    gated = (query * (long_part + gain * product)).astype(BF16).reshape(inner, steps, mine, sub)
-    for b in range(inner):
-        out_ref[:, :, b * sub : (b + 1) * sub] = gated[b]
+    for r in range(mine):
+        direct = spread(r, terms - 1, sub) * join([product[h][r] for h in range(per)], 1)
+        out_ref[r] = (join(query[r], 1) * (long_part[r * lags : (r + 1) * lags] + direct)).astype(BF16)
 
 
 def body(projections, taps, filter_spectra, skip_gain):
@@ -231,8 +233,7 @@
     forward, inverse = block_tables(sub)
     order = np.arange(lags).reshape(seq_count, inner).T.reshape(-1)
     across, woven, back = lag_tables(lags, order)
-    wh, wl = table(forward)
-    v = np.stack(table(inverse))
+    w, v = np.stack(table(forward[:tokens])), np.stack(table(inverse))
     ah, al = table(across)
     bh, bl = table(back)
     woven = np.concatenate(table(woven), axis=0)
@@ -249,18 +250,18 @@
         scratch_shapes=[
             pltpu.VMEM((streams, channels, tokens), BF16),
             pltpu.VMEM((count, streams, mine, tokens), BF16),
-            dma((streams,)),
-            dma,
+            dma((4,)),
+            dma((4,)),
         ],
         compiler_params=pltpu.CompilerParams(vmem_limit_bytes=8 << 20),
     )(fixed(projections))
     got = lax.all_to_all(sent, ("chan", "seq"), 0, 0, tiled=True)
-    tables = wh, lag
+    tables = w, lag
     ghat, scalars, *ready = pl.pallas_call(
         filter_kernel,
         out_shape=[
             jax.ShapeDtypeStruct((mine, 4 * lags, width), F32),
-            jax.ShapeDtypeStruct((streams * 3 + 1, 8, tokens), F32),
+            jax.ShapeDtypeStruct((mine * (streams * 3 + 1), 8, 128), F32),
         ]
         + [jax.ShapeDtypeStruct(t.shape, BF16) for t in tables],
         in_specs=[hbm] * 6,
@@ -275,15 +276,18 @@
         compiler_params=pltpu.CompilerParams(vmem_limit_bytes=12 << 20),
         cost_estimate=pl.CostEstimate(flops=1 << 28, bytes_accessed=4 << 20, transcendentals=0),
     )(*map(fixed, (filter_spectra, taps.transpose(0, 2, 1), skip_gain.reshape(1, channels), woven, *tables)))
+    rows = got.reshape(inner, per, seq_count, streams, mine, tokens).transpose(3, 4, 1, 0, 2, 5)
+    rows = rows.reshape(streams, mine, per, lags, tokens)
     out = pl.pallas_call(
         main_kernel,
-        out_shape=jax.ShapeDtypeStruct((seq_count, mine, length // seq_count), BF16),
-        in_specs=[vmem] * 5 + [hbm] * 2,
+        out_shape=jax.ShapeDtypeStruct((mine, lags, sub), BF16),
+        in_specs=[vmem] * 5 + [hbm],
         out_specs=vmem,
-        scratch_shapes=[pltpu.VMEM(wl.shape, BF16), pltpu.VMEM(v.shape, BF16), dma((3,))],
+        scratch_shapes=[pltpu.VMEM(v.shape, BF16), dma((2,))],
         compiler_params=pltpu.CompilerParams(vmem_limit_bytes=24 << 20),
         cost_estimate=pl.CostEstimate(flops=1 << 30, bytes_accessed=8 << 20, transcendentals=0),
-    )(got, ghat, scalars, *ready, fixed(wl), fixed(v))
+    )(rows, ghat, scalars, *ready, fixed(v))
+    out = out.reshape(mine, inner, seq_count, sub).transpose(2, 0, 1, 3).reshape(seq_count, mine, length // seq_count)
     out = lax.all_to_all(out, "seq", 0, 0, tiled=True)
     return out.reshape(local, length // seq_count)
 

time: 38.6 us -> 37.8 us (0.979)
  Pallas kernels: 7.6 us -> 6.42 us
    pallas_call x1, Pallas kernels: 3.36 us -> 2.27 us  [body(): pl.pallas_call(main_kernel, out_shape=jax.ShapeDtypeStruct((mine, lags, s...]
where the time goes in v5:
time: 37.8 us; the launch traced here: 37.5 us
  starting transfers between devices  11.1 us (29%)
  waiting for transfers between devices  9.9 us (26%)
  blocking collectives  8.97 us (24%)
  Pallas kernels  6.42 us (17%)
  local copies, waits for them, and re-layouts  1 us (3%)
    all_to_all x1, starting transfers between devices, body(): got = lax.all_to_all(sent, ('chan', 'seq'), 0, 0, tiled=True)  11.1 us
    all_to_all x1, waiting for transfers between devices, body(): got = lax.all_to_all(sent, ('chan', 'seq'), 0, 0, tiled=True)  9.9 us
    all_to_all x1, blocking collectives, body(): out = lax.all_to_all(out, 'seq', 0, 0, tiled=True)  8.97 us
    pallas_call x1, Pallas kernels, body(): pl.pallas_call(filter_kernel, out_shape=[jax.ShapeDtypeStruct((mine, 4 *...  2.38 us
    pallas_call x1, Pallas kernels, body(): pl.pallas_call(main_kernel, out_shape=jax.ShapeDtypeStruct((mine, lags, s...  2.27 us
    pallas_call x1, Pallas kernels, body(): pl.pallas_call(send_kernel, out_shape=jax.ShapeDtypeStruct((count, stream...  1.78 us
  transfers between devices with their start and end apart: 1, of which 1 were waited for; matrix products, arithmetic and copies ran while one was open for 0% of the time, Pallas kernels for 6%

profile of v5, /device:TPU:0, one launch (start us, length us, event | category | flops | bytes accessed | tf_op | source)
XLA Modules:
  0.0 37.5 jit_solution(7183676301832306536)
XLA Ops:
  0.0 1.8 %shard_map.82 = bf16[128,3,2,256]{3,2,1,0:T(2,128)(2,1)} custom-call(bf16[3,256,256]{2,1,0:T(8,128)(2,1)} %x_ref.1), custom_call_target="tpu_custom_call" | custom-call | tf_op jit(solution)/shard_map/pallas_call | solution.py:245
  1.8 11.1 %all-to-all-start = ((bf16[128,3,2,256]{3,2,1,0:T(2,128)(2,1)}), bf16[128,3,2,256]{3,2,1,0:T(2,128)(2,1)S(1)}, u32[]{:S(2)}, u32[]{:S(2)}) async-start(bf16[128,3,2,256]{3,2,1,0:T(2,128)(2,1)} %shard_map.82), calls=%async_computation | async-start | bytes 786432 | tf_op jit(solution)/shard_map/all_to_all | solution.py:258
  12.9 2.4 %shard_map.83 = (f32[2,256,640]{2,1,0:T(8,128)S(1)}, f32[20,8,128]{2,1,0:T(8,128)S(1)}, bf16[2,256,1024]{2,1,0:T(8,128)(2,1)S(1)}, bf16[768,256]{1,0:T(8,128)(2,1)S(1)}) custom-call(f32[16,64,2,1024]{3,2,1,0:T(2,128)} %g_hbm.1, f32[3,3,256]{2,1,0:T(4,128)} %bitcast.20, f32[1,256]{1,0:T(1,128)} %bitcast.21, bf16[512,128]{1,0:T(8,128)(2,1)} %constant.8.clone.lag_hbm, ...), custom_call_target="tpu_custom_call" | custom-call | flops 268435456 | bytes 4194304 | tf_op jit(solution)/shard_map/pallas_call | solution.py:260
  15.3 9.9 %all-to-all-done = bf16[128,3,2,256]{3,2,1,0:T(2,128)(2,1)S(1)} async-done(((bf16[128,3,2,256]{3,2,1,0:T(2,128)(2,1)}), bf16[128,3,2,256]{3,2,1,0:T(2,128)(2,1)S(1)}, u32[]{:S(2)}, u32[]{:S(2)}) %all-to-all-start) | async-done | bytes 393248 | tf_op jit(solution)/shard_map/all_to_all | solution.py:258
  25.3 2.3 %shard_map.84 = bf16[2,64,512]{2,1,0:T(8,128)(2,1)S(1)} custom-call(bf16[3,2,2,64,256]{4,3,2,1,0:T(8,128)(2,1)S(1)} %bitcast.16, f32[2,256,640]{2,1,0:T(8,128)S(1)} %get-tuple-element.9.ghat_ref, f32[20,8,128]{2,1,0:T(8,128)S(1)} %get-tuple-element.10.scal_ref, bf16[2,256,1024]{2,1,0:T(8,128)(2,1)S(1)} %get-tuple-element.11.w_ref, ...), custom_call_target="tpu_custom_call" | custom-call | flops 1073741824 | bytes 8388608 | tf_op jit(solution)/shard_map/pallas_call | solution.py:281
  27.6 0.1 reshape.22
  27.7 0.1 copy.17
  27.8 9.0 %all_to_all.10 = bf16[8,2,4096]{2,1,0:T(2,128)(2,1)S(1)} all-to-all(bf16[8,2,4096]{2,1,0:T(2,128)(2,1)S(1)} %copy.17), channel_id=1, replica_groups=mesh['seq'=8,'chan'=16] {'seq'}, dimensions={0} | all-to-all | bytes 262144 | tf_op jit(solution)/shard_map/all_to_all | solution.py:291
  36.8 0.7 %reshape.23 = bf16[16,4096]{1,0:T(8,128)(2,1)} reshape(bf16[8,2,4096]{2,1,0:T(2,128)(2,1)S(1)} %all_to_all.10) | data formatting | bytes 262144 | tf_op jit(solution)/shard_map/reshape | solution.py:292
  (2 shorter events, 0.1 us)
Async XLA Ops:
  1.8 23.4 %all-to-all-start = ((bf16[128,3,2,256]{3,2,1,0:T(2,128)(2,1)}), bf16[128,3,2,256]{3,2,1,0:T(2,128)(2,1)S(1)}, u32[]{:S(2)}, u32[]{:S(2)}) async-start(bf16[128,3,2,256]{3,2,1,0:T(2,128)(2,1)} %shard_map.82), calls=%async_computation | async-start | bytes 786432 | tf_op jit(solution)/shard_map/all_to_all | solution.py:258

commit v6 on v5

--- a/solution.py
+++ b/solution.py
@@ -214,7 +214,9 @@
     long_part = dot(mh, v_ref[0]) + dot(ml, v_ref[0]) + dot(mh, v_ref[1])
     for r in range(mine):
         direct = spread(r, terms - 1, sub) * join([product[h][r] for h in range(per)], 1)
-        out_ref[r] = (join(query[r], 1) * (long_part[r * lags : (r + 1) * lags] + direct)).astype(BF16)
+        gated = join(query[r], 1) * (long_part[r * lags : (r + 1) * lags] + direct)
+        for b in range(inner):
+            out_ref[r, :, b * sub : (b + 1) * sub] = gated[b * step : (b + 1) * step].astype(BF16)
 
 
 def body(projections, taps, filter_spectra, skip_gain):
@@ -280,15 +282,14 @@
     rows = rows.reshape(streams, mine, per, lags, tokens)
     out = pl.pallas_call(
         main_kernel,
-        out_shape=jax.ShapeDtypeStruct((mine, lags, sub), BF16),
+        out_shape=jax.ShapeDtypeStruct((mine, seq_count, length // seq_count), BF16),
         in_specs=[vmem] * 5 + [hbm],
         out_specs=vmem,
         scratch_shapes=[pltpu.VMEM(v.shape, BF16), dma((2,))],
         compiler_params=pltpu.CompilerParams(vmem_limit_bytes=24 << 20),
         cost_estimate=pl.CostEstimate(flops=1 << 30, bytes_accessed=8 << 20, transcendentals=0),
     )(rows, ghat, scalars, *ready, fixed(v))
-    out = out.reshape(mine, inner, seq_count, sub).transpose(2, 0, 1, 3).reshape(seq_count, mine, length // seq_count)
-    out = lax.all_to_all(out, "seq", 0, 0, tiled=True)
+    out = lax.all_to_all(out.transpose(1, 0, 2), "seq", 0, 0, tiled=True)
     return out.reshape(local, length // seq_count)
 
 

time: 37.8 us -> 37.6 us (level)
  no operation moved by 1% of the time
where the time goes in v6:
time: 37.6 us; the launch traced here: 37.4 us
  starting transfers between devices  11.1 us (30%)
  waiting for transfers between devices  9.9 us (26%)
  blocking collectives  8.97 us (24%)
  Pallas kernels  6.42 us (17%)
  local copies, waits for them, and re-layouts  0.89 us (2%)
    all_to_all x1, starting transfers between devices, body(): got = lax.all_to_all(sent, ('chan', 'seq'), 0, 0, tiled=True)  11.1 us
    all_to_all x1, waiting for transfers between devices, body(): got = lax.all_to_all(sent, ('chan', 'seq'), 0, 0, tiled=True)  9.9 us
    all_to_all x1, blocking collectives, body(): out = lax.all_to_all(out.transpose(1, 0, 2), 'seq', 0, 0, tiled=True)  8.97 us
    pallas_call x1, Pallas kernels, body(): pl.pallas_call(filter_kernel, out_shape=[jax.ShapeDtypeStruct((mine, 4 *...  2.38 us
    pallas_call x1, Pallas kernels, body(): pl.pallas_call(main_kernel, out_shape=jax.ShapeDtypeStruct((mine, seq_cou...  2.27 us
    pallas_call x1, Pallas kernels, body(): pl.pallas_call(send_kernel, out_shape=jax.ShapeDtypeStruct((count, stream...  1.78 us
  transfers between devices with their start and end apart: 1, of which 1 were waited for; matrix products, arithmetic and copies ran while one was open for 0% of the time, Pallas kernels for 6%

profile of v6, /device:TPU:0, one launch (start us, length us, event | category | flops | bytes accessed | tf_op | source)
XLA Modules:
  0.0 37.4 jit_solution(13684100704452998914)
XLA Ops:
  0.0 1.8 %shard_map.82 = bf16[128,3,2,256]{3,2,1,0:T(2,128)(2,1)} custom-call(bf16[3,256,256]{2,1,0:T(8,128)(2,1)} %x_ref.1), custom_call_target="tpu_custom_call" | custom-call | tf_op jit(solution)/shard_map/pallas_call | solution.py:247
  1.8 11.1 %all-to-all-start = ((bf16[128,3,2,256]{3,2,1,0:T(2,128)(2,1)}), bf16[128,3,2,256]{3,2,1,0:T(2,128)(2,1)S(1)}, u32[]{:S(2)}, u32[]{:S(2)}) async-start(bf16[128,3,2,256]{3,2,1,0:T(2,128)(2,1)} %shard_map.82), calls=%async_computation | async-start | bytes 786432 | tf_op jit(solution)/shard_map/all_to_all | solution.py:260
  12.9 2.4 %shard_map.83 = (f32[2,256,640]{2,1,0:T(8,128)S(1)}, f32[20,8,128]{2,1,0:T(8,128)S(1)}, bf16[2,256,1024]{2,1,0:T(8,128)(2,1)S(1)}, bf16[768,256]{1,0:T(8,128)(2,1)S(1)}) custom-call(f32[16,64,2,1024]{3,2,1,0:T(2,128)} %g_hbm.1, f32[3,3,256]{2,1,0:T(4,128)} %bitcast.12, f32[1,256]{1,0:T(1,128)} %bitcast.13, bf16[512,128]{1,0:T(8,128)(2,1)} %constant.8.clone.lag_hbm, ...), custom_call_target="tpu_custom_call" | custom-call | flops 268435456 | bytes 4194304 | tf_op jit(solution)/shard_map/pallas_call | solution.py:262
  15.3 9.9 %all-to-all-done = bf16[128,3,2,256]{3,2,1,0:T(2,128)(2,1)S(1)} async-done(((bf16[128,3,2,256]{3,2,1,0:T(2,128)(2,1)}), bf16[128,3,2,256]{3,2,1,0:T(2,128)(2,1)S(1)}, u32[]{:S(2)}, u32[]{:S(2)}) %all-to-all-start) | async-done | bytes 393248 | tf_op jit(solution)/shard_map/all_to_all | solution.py:260
  25.3 2.3 %shard_map.84 = bf16[2,8,4096]{2,1,0:T(8,128)(2,1)S(1)} custom-call(bf16[3,2,2,64,256]{4,3,2,1,0:T(8,128)(2,1)S(1)} %bitcast.9, f32[2,256,640]{2,1,0:T(8,128)S(1)} %get-tuple-element.9.ghat_ref, f32[20,8,128]{2,1,0:T(8,128)S(1)} %get-tuple-element.10.scal_ref, bf16[2,256,1024]{2,1,0:T(8,128)(2,1)S(1)} %get-tuple-element.11.w_ref, ...), custom_call_target="tpu_custom_call" | custom-call | flops 1073741824 | bytes 8388608 | tf_op jit(solution)/shard_map/pallas_call | solution.py:283
  27.6 0.1 copy.13
  27.7 9.0 %all_to_all.10 = bf16[8,2,4096]{2,1,0:T(2,128)(2,1)S(1)} all-to-all(bf16[8,2,4096]{2,1,0:T(2,128)(2,1)S(1)} %copy.13), channel_id=1, replica_groups=mesh['seq'=8,'chan'=16] {'seq'}, dimensions={0} | all-to-all | bytes 262144 | tf_op jit(solution)/shard_map/all_to_all | solution.py:292
  36.7 0.7 %reshape.15 = bf16[16,4096]{1,0:T(8,128)(2,1)} reshape(bf16[8,2,4096]{2,1,0:T(2,128)(2,1)S(1)} %all_to_all.10) | data formatting | bytes 262144 | tf_op jit(solution)/shard_map/reshape | solution.py:293
  (1 shorter events, 0.0 us)
Async XLA Ops:
  1.8 23.4 %all-to-all-start = ((bf16[128,3,2,256]{3,2,1,0:T(2,128)(2,1)}), bf16[128,3,2,256]{3,2,1,0:T(2,128)(2,1)S(1)}, u32[]{:S(2)}, u32[]{:S(2)}) async-start(bf16[128,3,2,256]{3,2,1,0:T(2,128)(2,1)} %shard_map.82), calls=%async_computation | async-start | bytes 786432 | tf_op jit(solution)/shard_map/all_to_all | solution.py:260

commit v7 on v5

--- a/solution.py
+++ b/solution.py
@@ -209,9 +209,10 @@
         tail = mixed[lags:, mine * sub + r * 128 : mine * sub + (r + 1) * 128]
         parts.append(join([real, jnp.where(zero, tail, imag[:, :128]), imag[:, 128:]], 1))
     mh, ml = halves(join(parts, 0))
-    for copy in copies:
-        copy.wait()
-    long_part = dot(mh, v_ref[0]) + dot(ml, v_ref[0]) + dot(mh, v_ref[1])
+    copies[0].wait()
+    long_part = dot(mh, v_ref[0]) + dot(ml, v_ref[0])
+    copies[1].wait()
+    long_part = long_part + dot(mh, v_ref[1])
     for r in range(mine):
         direct = spread(r, terms - 1, sub) * join([product[h][r] for h in range(per)], 1)
         out_ref[r] = (join(query[r], 1) * (long_part[r * lags : (r + 1) * lags] + direct)).astype(BF16)

time: 37.8 us -> 37.8 us (level)
  no operation moved by 1% of the time
where the time goes in v7:
time: 37.8 us; the launch traced here: 37.6 us
  starting transfers between devices  11.1 us (29%)
  waiting for transfers between devices  9.9 us (26%)
  blocking collectives  8.97 us (24%)
  Pallas kernels  6.48 us (17%)
  local copies, waits for them, and re-layouts  1 us (3%)
    all_to_all x1, starting transfers between devices, body(): got = lax.all_to_all(sent, ('chan', 'seq'), 0, 0, tiled=True)  11.1 us
    all_to_all x1, waiting for transfers between devices, body(): got = lax.all_to_all(sent, ('chan', 'seq'), 0, 0, tiled=True)  9.9 us
    all_to_all x1, blocking collectives, body(): out = lax.all_to_all(out, 'seq', 0, 0, tiled=True)  8.97 us
    pallas_call x1, Pallas kernels, body(): pl.pallas_call(filter_kernel, out_shape=[jax.ShapeDtypeStruct((mine, 4 *...  2.38 us
    pallas_call x1, Pallas kernels, body(): pl.pallas_call(main_kernel, out_shape=jax.ShapeDtypeStruct((mine, lags, s...  2.33 us
    pallas_call x1, Pallas kernels, body(): pl.pallas_call(send_kernel, out_shape=jax.ShapeDtypeStruct((count, stream...  1.78 us
  transfers between devices with their start and end apart: 1, of which 1 were waited for; matrix products, arithmetic and copies ran while one was open for 0% of the time, Pallas kernels for 6%

profile of v7, /device:TPU:0, one launch (start us, length us, event | category | flops | bytes accessed | tf_op | source)
XLA Modules:
  0.0 37.6 jit_solution(6159741728596050255)
XLA Ops:
  0.0 1.8 %shard_map.82 = bf16[128,3,2,256]{3,2,1,0:T(2,128)(2,1)} custom-call(bf16[3,256,256]{2,1,0:T(8,128)(2,1)} %x_ref.1), custom_call_target="tpu_custom_call" | custom-call | tf_op jit(solution)/shard_map/pallas_call | solution.py:246
  1.8 11.1 %all-to-all-start = ((bf16[128,3,2,256]{3,2,1,0:T(2,128)(2,1)}), bf16[128,3,2,256]{3,2,1,0:T(2,128)(2,1)S(1)}, u32[]{:S(2)}, u32[]{:S(2)}) async-start(bf16[128,3,2,256]{3,2,1,0:T(2,128)(2,1)} %shard_map.82), calls=%async_computation | async-start | bytes 786432 | tf_op jit(solution)/shard_map/all_to_all | solution.py:259
  12.9 2.4 %shard_map.83 = (f32[2,256,640]{2,1,0:T(8,128)S(1)}, f32[20,8,128]{2,1,0:T(8,128)S(1)}, bf16[2,256,1024]{2,1,0:T(8,128)(2,1)S(1)}, bf16[768,256]{1,0:T(8,128)(2,1)S(1)}) custom-call(f32[16,64,2,1024]{3,2,1,0:T(2,128)} %g_hbm.1, f32[3,3,256]{2,1,0:T(4,128)} %bitcast.20, f32[1,256]{1,0:T(1,128)} %bitcast.21, bf16[512,128]{1,0:T(8,128)(2,1)} %constant.8.clone.lag_hbm, ...), custom_call_target="tpu_custom_call" | custom-call | flops 268435456 | bytes 4194304 | tf_op jit(solution)/shard_map/pallas_call | solution.py:261
  15.3 9.9 %all-to-all-done = bf16[128,3,2,256]{3,2,1,0:T(2,128)(2,1)S(1)} async-done(((bf16[128,3,2,256]{3,2,1,0:T(2,128)(2,1)}), bf16[128,3,2,256]{3,2,1,0:T(2,128)(2,1)S(1)}, u32[]{:S(2)}, u32[]{:S(2)}) %all-to-all-start) | async-done | bytes 393248 | tf_op jit(solution)/shard_map/all_to_all | solution.py:259
  25.3 2.3 %shard_map.84 = bf16[2,64,512]{2,1,0:T(8,128)(2,1)S(1)} custom-call(bf16[3,2,2,64,256]{4,3,2,1,0:T(8,128)(2,1)S(1)} %bitcast.16, f32[2,256,640]{2,1,0:T(8,128)S(1)} %get-tuple-element.9.ghat_ref, f32[20,8,128]{2,1,0:T(8,128)S(1)} %get-tuple-element.10.scal_ref, bf16[2,256,1024]{2,1,0:T(8,128)(2,1)S(1)} %get-tuple-element.11.w_ref, ...), custom_call_target="tpu_custom_call" | custom-call | flops 1073741824 | bytes 8388608 | tf_op jit(solution)/shard_map/pallas_call | solution.py:282
  27.7 0.1 reshape.22
  27.7 0.1 copy.17
  27.9 9.0 %all_to_all.10 = bf16[8,2,4096]{2,1,0:T(2,128)(2,1)S(1)} all-to-all(bf16[8,2,4096]{2,1,0:T(2,128)(2,1)S(1)} %copy.17), channel_id=1, replica_groups=mesh['seq'=8,'chan'=16] {'seq'}, dimensions={0} | all-to-all | bytes 262144 | tf_op jit(solution)/shard_map/all_to_all | solution.py:292
  36.9 0.7 %reshape.23 = bf16[16,4096]{1,0:T(8,128)(2,1)} reshape(bf16[8,2,4096]{2,1,0:T(2,128)(2,1)S(1)} %all_to_all.10) | data formatting | bytes 262144 | tf_op jit(solution)/shard_map/reshape | solution.py:293
  (2 shorter events, 0.1 us)
Async XLA Ops:
  1.8 23.4 %all-to-all-start = ((bf16[128,3,2,256]{3,2,1,0:T(2,128)(2,1)}), bf16[128,3,2,256]{3,2,1,0:T(2,128)(2,1)S(1)}, u32[]{:S(2)}, u32[]{:S(2)}) async-start(bf16[128,3,2,256]{3,2,1,0:T(2,128)(2,1)} %shard_map.82), calls=%async_computation | async-start | bytes 786432 | tf_op jit(solution)/shard_map/all_to_all | solution.py:259

commit v8 on v7

--- a/solution.py
+++ b/solution.py
@@ -215,7 +215,9 @@
     long_part = long_part + dot(mh, v_ref[1])
     for r in range(mine):
         direct = spread(r, terms - 1, sub) * join([product[h][r] for h in range(per)], 1)
-        out_ref[r] = (join(query[r], 1) * (long_part[r * lags : (r + 1) * lags] + direct)).astype(BF16)
+        gated = join(query[r], 1) * (long_part[r * lags : (r + 1) * lags] + direct)
+        for b in range(inner):
+            out_ref[r, :, b * sub : (b + 1) * sub] = gated[b * step : (b + 1) * step]
 
 
 def body(projections, taps, filter_spectra, skip_gain):
@@ -281,15 +283,14 @@
     rows = rows.reshape(streams, mine, per, lags, tokens)
     out = pl.pallas_call(
         main_kernel,
-        out_shape=jax.ShapeDtypeStruct((mine, lags, sub), BF16),
+        out_shape=jax.ShapeDtypeStruct((mine, seq_count, length // seq_count), F32),
         in_specs=[vmem] * 5 + [hbm],
         out_specs=vmem,
         scratch_shapes=[pltpu.VMEM(v.shape, BF16), dma((2,))],
         compiler_params=pltpu.CompilerParams(vmem_limit_bytes=24 << 20),
         cost_estimate=pl.CostEstimate(flops=1 << 30, bytes_accessed=8 << 20, transcendentals=0),
     )(rows, ghat, scalars, *ready, fixed(v))
-    out = out.reshape(mine, inner, seq_count, sub).transpose(2, 0, 1, 3).reshape(seq_count, mine, length // seq_count)
-    out = lax.all_to_all(out, "seq", 0, 0, tiled=True)
+    out = lax.all_to_all(out.astype(BF16).transpose(1, 0, 2), "seq", 0, 0, tiled=True)
     return out.reshape(local, length // seq_count)
 
 

time: 37.8 us -> 37.7 us (level)
  no operation moved by 1% of the time
where the time goes in v8:
time: 37.7 us; the launch traced here: 37.5 us
  starting transfers between devices  11.1 us (29%)
  waiting for transfers between devices  9.9 us (26%)
  blocking collectives  8.97 us (24%)
  Pallas kernels  6.48 us (17%)
  local copies, waits for them, and re-layouts  0.89 us (2%)
    all_to_all x1, starting transfers between devices, body(): got = lax.all_to_all(sent, ('chan', 'seq'), 0, 0, tiled=True)  11.1 us
    all_to_all x1, waiting for transfers between devices, body(): got = lax.all_to_all(sent, ('chan', 'seq'), 0, 0, tiled=True)  9.9 us
    all_to_all x1, blocking collectives, body(): lax.all_to_all(out.astype(BF16).transpose(1, 0, 2), 'seq', 0, 0, tiled=True)  8.97 us
    pallas_call x1, Pallas kernels, body(): pl.pallas_call(filter_kernel, out_shape=[jax.ShapeDtypeStruct((mine, 4 *...  2.38 us
    pallas_call x1, Pallas kernels, body(): pl.pallas_call(main_kernel, out_shape=jax.ShapeDtypeStruct((mine, seq_cou...  2.33 us
    pallas_call x1, Pallas kernels, body(): pl.pallas_call(send_kernel, out_shape=jax.ShapeDtypeStruct((count, stream...  1.78 us
  transfers between devices with their start and end apart: 1, of which 1 were waited for; matrix products, arithmetic and copies ran while one was open for 0% of the time, Pallas kernels for 6%

profile of v8, /device:TPU:0, one launch (start us, length us, event | category | flops | bytes accessed | tf_op | source)
XLA Modules:
  0.0 37.5 jit_solution(14675070066297853574)
XLA Ops:
  0.0 1.8 %shard_map.82 = bf16[128,3,2,256]{3,2,1,0:T(2,128)(2,1)} custom-call(bf16[3,256,256]{2,1,0:T(8,128)(2,1)} %x_ref.1), custom_call_target="tpu_custom_call" | custom-call | tf_op jit(solution)/shard_map/pallas_call | solution.py:248
  1.8 11.1 %all-to-all-start = ((bf16[128,3,2,256]{3,2,1,0:T(2,128)(2,1)}), bf16[128,3,2,256]{3,2,1,0:T(2,128)(2,1)S(1)}, u32[]{:S(2)}, u32[]{:S(2)}) async-start(bf16[128,3,2,256]{3,2,1,0:T(2,128)(2,1)} %shard_map.82), calls=%async_computation | async-start | bytes 786432 | tf_op jit(solution)/shard_map/all_to_all | solution.py:261
  12.9 2.4 %shard_map.83 = (f32[2,256,640]{2,1,0:T(8,128)S(1)}, f32[20,8,128]{2,1,0:T(8,128)S(1)}, bf16[2,256,1024]{2,1,0:T(8,128)(2,1)S(1)}, bf16[768,256]{1,0:T(8,128)(2,1)S(1)}) custom-call(f32[16,64,2,1024]{3,2,1,0:T(2,128)} %g_hbm.1, f32[3,3,256]{2,1,0:T(4,128)} %bitcast.12, f32[1,256]{1,0:T(1,128)} %bitcast.13, bf16[512,128]{1,0:T(8,128)(2,1)} %constant.8.clone.lag_hbm, ...), custom_call_target="tpu_custom_call" | custom-call | flops 268435456 | bytes 4194304 | tf_op jit(solution)/shard_map/pallas_call | solution.py:263
  15.3 9.9 %all-to-all-done = bf16[128,3,2,256]{3,2,1,0:T(2,128)(2,1)S(1)} async-done(((bf16[128,3,2,256]{3,2,1,0:T(2,128)(2,1)}), bf16[128,3,2,256]{3,2,1,0:T(2,128)(2,1)S(1)}, u32[]{:S(2)}, u32[]{:S(2)}) %all-to-all-start) | async-done | bytes 393248 | tf_op jit(solution)/shard_map/all_to_all | solution.py:261
  25.3 2.3 %shard_map.84 = f32[2,8,4096]{2,1,0:T(8,128)S(1)} custom-call(bf16[3,2,2,64,256]{4,3,2,1,0:T(8,128)(2,1)S(1)} %bitcast.10, f32[2,256,640]{2,1,0:T(8,128)S(1)} %get-tuple-element.9.ghat_ref, f32[20,8,128]{2,1,0:T(8,128)S(1)} %get-tuple-element.10.scal_ref, bf16[2,256,1024]{2,1,0:T(8,128)(2,1)S(1)} %get-tuple-element.11.w_ref, ...), custom_call_target="tpu_custom_call" | custom-call | flops 1073741824 | bytes 8388608 | tf_op jit(solution)/shard_map/pallas_call | solution.py:284
  27.6 0.1 copy.13
  27.8 9.0 %all_to_all.10 = bf16[8,2,4096]{2,1,0:T(2,128)(2,1)S(1)} all-to-all(bf16[8,2,4096]{2,1,0:T(2,128)(2,1)S(1)} %copy.13), channel_id=1, replica_groups=mesh['seq'=8,'chan'=16] {'seq'}, dimensions={0} | all-to-all | bytes 262144 | tf_op jit(solution)/shard_map/all_to_all | solution.py:293
  36.8 0.7 %reshape.15 = bf16[16,4096]{1,0:T(8,128)(2,1)} reshape(bf16[8,2,4096]{2,1,0:T(2,128)(2,1)S(1)} %all_to_all.10) | data formatting | bytes 262144 | tf_op jit(solution)/shard_map/reshape | solution.py:294
  (2 shorter events, 0.1 us)
Async XLA Ops:
  1.8 23.4 %all-to-all-start = ((bf16[128,3,2,256]{3,2,1,0:T(2,128)(2,1)}), bf16[128,3,2,256]{3,2,1,0:T(2,128)(2,1)S(1)}, u32[]{:S(2)}, u32[]{:S(2)}) async-start(bf16[128,3,2,256]{3,2,1,0:T(2,128)(2,1)} %shard_map.82), calls=%async_computation | async-start | bytes 786432 | tf_op jit(solution)/shard_map/all_to_all | solution.py:261

commit v9 on v5

--- a/solution.py
+++ b/solution.py
@@ -250,8 +250,8 @@
         scratch_shapes=[
             pltpu.VMEM((streams, channels, tokens), BF16),
             pltpu.VMEM((count, streams, mine, tokens), BF16),
-            dma((4,)),
-            dma((4,)),
+            dma((8,)),
+            dma((8,)),
         ],
         compiler_params=pltpu.CompilerParams(vmem_limit_bytes=8 << 20),
     )(fixed(projections))

time: 37.8 us -> 37.8 us (level)
  no operation moved by 1% of the time
where the time goes in v9:
time: 37.8 us; the launch traced here: 37.5 us
  starting transfers between devices  11.1 us (29%)
  waiting for transfers between devices  9.9 us (26%)
  blocking collectives  8.97 us (24%)
  Pallas kernels  6.4 us (17%)
  local copies, waits for them, and re-layouts  1 us (3%)
    all_to_all x1, starting transfers between devices, body(): got = lax.all_to_all(sent, ('chan', 'seq'), 0, 0, tiled=True)  11.1 us
    all_to_all x1, waiting for transfers between devices, body(): got = lax.all_to_all(sent, ('chan', 'seq'), 0, 0, tiled=True)  9.9 us
    all_to_all x1, blocking collectives, body(): out = lax.all_to_all(out, 'seq', 0, 0, tiled=True)  8.97 us
    pallas_call x1, Pallas kernels, body(): pl.pallas_call(filter_kernel, out_shape=[jax.ShapeDtypeStruct((mine, 4 *...  2.38 us
    pallas_call x1, Pallas kernels, body(): pl.pallas_call(main_kernel, out_shape=jax.ShapeDtypeStruct((mine, lags, s...  2.28 us
    pallas_call x1, Pallas kernels, body(): pl.pallas_call(send_kernel, out_shape=jax.ShapeDtypeStruct((count, stream...  1.74 us
  transfers between devices with their start and end apart: 1, of which 1 were waited for; matrix products, arithmetic and copies ran while one was open for 0% of the time, Pallas kernels for 6%

profile of v9, /device:TPU:0, one launch (start us, length us, event | category | flops | bytes accessed | tf_op | source)
XLA Modules:
  0.0 37.5 jit_solution(3745591797511277415)
XLA Ops:
  0.0 1.7 %shard_map.82 = bf16[128,3,2,256]{3,2,1,0:T(2,128)(2,1)} custom-call(bf16[3,256,256]{2,1,0:T(8,128)(2,1)} %x_ref.1), custom_call_target="tpu_custom_call" | custom-call | tf_op jit(solution)/shard_map/pallas_call | solution.py:245
  1.8 11.1 %all-to-all-start = ((bf16[128,3,2,256]{3,2,1,0:T(2,128)(2,1)}), bf16[128,3,2,256]{3,2,1,0:T(2,128)(2,1)S(1)}, u32[]{:S(2)}, u32[]{:S(2)}) async-start(bf16[128,3,2,256]{3,2,1,0:T(2,128)(2,1)} %shard_map.82), calls=%async_computation | async-start | bytes 786432 | tf_op jit(solution)/shard_map/all_to_all | solution.py:258
  12.9 2.4 %shard_map.83 = (f32[2,256,640]{2,1,0:T(8,128)S(1)}, f32[20,8,128]{2,1,0:T(8,128)S(1)}, bf16[2,256,1024]{2,1,0:T(8,128)(2,1)S(1)}, bf16[768,256]{1,0:T(8,128)(2,1)S(1)}) custom-call(f32[16,64,2,1024]{3,2,1,0:T(2,128)} %g_hbm.1, f32[3,3,256]{2,1,0:T(4,128)} %bitcast.20, f32[1,256]{1,0:T(1,128)} %bitcast.21, bf16[512,128]{1,0:T(8,128)(2,1)} %constant.8.clone.lag_hbm, ...), custom_call_target="tpu_custom_call" | custom-call | flops 268435456 | bytes 4194304 | tf_op jit(solution)/shard_map/pallas_call | solution.py:260
  15.3 9.9 %all-to-all-done = bf16[128,3,2,256]{3,2,1,0:T(2,128)(2,1)S(1)} async-done(((bf16[128,3,2,256]{3,2,1,0:T(2,128)(2,1)}), bf16[128,3,2,256]{3,2,1,0:T(2,128)(2,1)S(1)}, u32[]{:S(2)}, u32[]{:S(2)}) %all-to-all-start) | async-done | bytes 393248 | tf_op jit(solution)/shard_map/all_to_all | solution.py:258
  25.2 2.3 %shard_map.84 = bf16[2,64,512]{2,1,0:T(8,128)(2,1)S(1)} custom-call(bf16[3,2,2,64,256]{4,3,2,1,0:T(8,128)(2,1)S(1)} %bitcast.16, f32[2,256,640]{2,1,0:T(8,128)S(1)} %get-tuple-element.9.ghat_ref, f32[20,8,128]{2,1,0:T(8,128)S(1)} %get-tuple-element.10.scal_ref, bf16[2,256,1024]{2,1,0:T(8,128)(2,1)S(1)} %get-tuple-element.11.w_ref, ...), custom_call_target="tpu_custom_call" | custom-call | flops 1073741824 | bytes 8388608 | tf_op jit(solution)/shard_map/pallas_call | solution.py:281
  27.6 0.1 reshape.22
  27.7 0.1 copy.17
  27.8 9.0 %all_to_all.10 = bf16[8,2,4096]{2,1,0:T(2,128)(2,1)S(1)} all-to-all(bf16[8,2,4096]{2,1,0:T(2,128)(2,1)S(1)} %copy.17), channel_id=1, replica_groups=mesh['seq'=8,'chan'=16] {'seq'}, dimensions={0} | all-to-all | bytes 262144 | tf_op jit(solution)/shard_map/all_to_all | solution.py:291
  36.8 0.7 %reshape.23 = bf16[16,4096]{1,0:T(8,128)(2,1)} reshape(bf16[8,2,4096]{2,1,0:T(2,128)(2,1)S(1)} %all_to_all.10) | data formatting | bytes 262144 | tf_op jit(solution)/shard_map/reshape | solution.py:292
  (2 shorter events, 0.1 us)
Async XLA Ops:
  1.8 23.4 %all-to-all-start = ((bf16[128,3,2,256]{3,2,1,0:T(2,128)(2,1)}), bf16[128,3,2,256]{3,2,1,0:T(2,128)(2,1)S(1)}, u32[]{:S(2)}, u32[]{:S(2)}) async-start(bf16[128,3,2,256]{3,2,1,0:T(2,128)(2,1)} %shard_map.82), calls=%async_computation | async-start | bytes 786432 | tf_op jit(solution)/shard_map/all_to_all | solution.py:258
